TPU v7x, 128 devices: a whole 4x4x4 slice. The times are simulated.
128 devices in a mesh: seq: 32 (over x, y_lo, z), tp: 4 (over y_hi, core).
Axes of the slice: x: 4, y: 4 (y_hi: 2, y_lo: 2; y = y_hi * 2 + y_lo), z: 4, core: 2. Of those that a mesh axis runs over, the one named last changes fastest.
Arguments:
- query_heads: bfloat16 [8192, 2048], P('seq', 'tp'), may hold values from -96 to 96
- key_heads: bfloat16 [8192, 2048], P('seq', 'tp'), may hold values from -4 to 4
- value_heads: bfloat16 [8192, 2048], P('seq', 'tp'), may hold values from -6 to 6
- residual: bfloat16 [8192, 4096], P('seq'), may hold values from -64 to 64
- out_weight: bfloat16 [2048, 4096], P('tp'), may hold values from -0.125 to 0.125
- ln_gain: float32 [4096], replicated, may hold values from 0.1 to 1.9
- up_source: bfloat16 [4096, 4096], P(None, 'tp'), may hold values from -0.09375 to 0.09375
- down_source: bfloat16 [4096, 4096], P('tp'), may hold values from -0.09375 to 0.09375
- copy_gain: float32 [4096], P('tp'), may hold values from 0.3 to 3
- neuron_source: int32 [4096], P('tp'), may hold values from 0 to 4095, as said below
- cotangent: bfloat16 [8192, 4096], P('seq'), may hold values from -6 to 6
Outputs:
- encoded: float32 [8192, 4096], P(('seq', 'tp'))
- grad_query: float32 [8192, 2048], P('seq', 'tp')
- grad_key: float32 [8192, 2048], P('seq', 'tp')
- grad_value: float32 [8192, 2048], P('seq', 'tp')
- grad_residual: float32 [8192, 4096], P('seq', 'tp')
Inputs may be any that keep to these rules, and one draw needn't show every extreme that they name: Added neuron j splits a source neuron of its own group: neuron_source[j] // 1024 == j // 1024.
All inputs are finite; a program needn't handle non-finite values.
Results may differ from a plain program's by a relative error of at most 0.035.
Values may be sent and summed in bfloat16 or wider, within the bound.
No kernel may reach another device: no remote copies, remote signals or barrier semaphores. Data moves between devices by JAX's collectives and lax.ppermute only.
A program may use at most 128 MiB of HBM per device.

v0:
```python
import functools
import math

import jax
import jax.numpy as jnp
from jax import lax
from jax.experimental import pallas as pl
from jax.experimental.pallas import tpu as pltpu
from jax.sharding import PartitionSpec as P

HEAD_DIM = 128
EPSILON = 1e-05
LOG2E = math.log2(math.e)
F32 = jnp.float32
BF16 = jnp.bfloat16
NT = (((1,), (1,)), ((), ()))
STAT_ROWS = 16
VMEM_LIMIT = 16 * 1024 * 1024
OUT_STEP = 512
NORM_STEP = 512
COST = 1024

VMEM = pl.BlockSpec(memory_space=pltpu.VMEM)
SMEM = pl.BlockSpec(memory_space=pltpu.SMEM)


def call(kernel, out_shape, in_specs, scratch=()):
    return pl.pallas_call(
        kernel,
        out_shape=out_shape,
        in_specs=in_specs,
        out_specs=jax.tree.map(lambda _: VMEM, out_shape),
        scratch_shapes=list(scratch),
        compiler_params=pltpu.CompilerParams(vmem_limit_bytes=VMEM_LIMIT),
        cost_estimate=pl.CostEstimate(flops=COST, bytes_accessed=COST, transcendentals=0),
    )


def shape(dims, dtype):
    return jax.ShapeDtypeStruct(dims, dtype)


def dot(a, b):
    return jnp.dot(a, b, preferred_element_type=F32)


def dot_nt(a, b):
    return lax.dot_general(a, b, NT, preferred_element_type=F32)


def swap_core(array):
    return lax.ppermute(array, "tp", [(0, 1), (1, 0), (2, 3), (3, 2)])


def swap_chip(array):
    return lax.ppermute(array, "tp", [(0, 2), (2, 0), (1, 3), (3, 1)])


def after(value, *earlier):
    return lax.optimization_barrier((value, earlier))[0]


def swap_block(array, first):
    count = lax.axis_size("seq")
    ahead = [(i, i + 1) for i in range(first, count - 1, 2)]
    return lax.ppermute(array, "seq", ahead + [(j, i) for i, j in ahead])


def nearby_offsets(seq):
    side = 2 * (seq % 2) - 1
    return side, -side, 2 * side, -2 * side


def three_parts(values):
    high = values.astype(BF16).astype(F32)
    middle = (values - high).astype(BF16).astype(F32)
    low = values - high - middle
    return high, middle, low


def stat_rows(columns, heads):
    rows = columns.T[:heads]
    parts = three_parts(rows)
    fill = jnp.zeros((STAT_ROWS - 3 * heads, rows.shape[1]), F32)
    return jnp.concatenate(parts + (fill,), axis=0).astype(BF16)


def read_stat(pack, head, heads, rows):
    block = pack[rows : rows + STAT_ROWS, :rows].astype(F32)
    line = lax.broadcasted_iota(jnp.int32, block.shape, 0)
    chosen = (line % heads == head) & (line < 3 * heads)
    return jnp.sum(jnp.where(chosen, block, 0.0), axis=0, keepdims=True)


def head_columns(head):
    return pl.ds(pl.multiple_of(head * HEAD_DIM, HEAD_DIM), HEAD_DIM)


def pick_lane(columns, lane):
    lanes = lax.broadcasted_iota(jnp.int32, columns.shape, 1)
    return jnp.sum(jnp.where(lanes == lane, columns, 0.0), axis=1, keepdims=True)


def local_starts(core, rows):
    slab = rows // 4
    return [(2 * part + (core if own else 1 - core)) * slab for own in (True, False) for part in range(2)]


def attention_kernel(scale, place, q_ref, *refs):
    key_refs, value_refs = refs[0:10:2], refs[1:10:2]
    att_ref, pack_ref, lse_ref = refs[10:]
    rows, width = q_ref.shape
    heads = width // HEAD_DIM
    slab = rows // 4
    seq, blocks, core = place[0], place[1], place[2]
    for index, start in enumerate(local_starts(core, rows)):
        pack_ref[index * slab : (index + 1) * slab] = q_ref[pl.ds(start, slab)]
    lane = lax.broadcasted_iota(jnp.int32, (rows, HEAD_DIM), 1)
    lse_all = jnp.zeros((rows, HEAD_DIM), F32)
    for head in range(heads):
        cols = slice(head * HEAD_DIM, (head + 1) * HEAD_DIM)
        query = pack_ref[:rows, cols]
        scores = []
        values = []
        for index, offset in enumerate((0,) + nearby_offsets(seq)):
            values.append(value_refs[index][:, cols])
            score = dot_nt(query, key_refs[index][:, cols]) * (scale * LOG2E)
            if index > 0:
                valid = (seq + offset >= 0) & (seq + offset < blocks)
                score = jnp.where(valid, score, -1e30)
            scores.append(score)
        top = scores[0]
        for score in scores[1:]:
            top = jnp.maximum(top, score)
        top = jnp.max(top, axis=1, keepdims=True)
        total = jnp.zeros((rows, rows), F32)
        mixed = jnp.zeros((rows, HEAD_DIM), F32)
        for score, value in zip(scores, values):
            weight = jnp.exp2(score - top)
            total = total + weight
            mixed = mixed + dot(weight.astype(BF16), value)
        total = jnp.sum(total, axis=1, keepdims=True)
        att_ref[:, cols] = (mixed / total).astype(BF16)
        lse_all = jnp.where(lane == head, top + jnp.log2(total), lse_all)
    lse_ref[...] = lse_all
    pack_ref[rows:, :rows] = stat_rows(lse_all, heads)
    pack_ref[rows:, rows:] = jnp.zeros((STAT_ROWS, width - rows), BF16)


def out_kernel(att_ref, weight_ref, own_ref, other_ref):
    rows, width = own_ref.shape
    for start in range(0, width, OUT_STEP):
        product = dot(att_ref[...], weight_ref[:, start : start + OUT_STEP]).astype(BF16)
        own_ref[:, start : start + OUT_STEP] = product[:rows]
        other_ref[:, start : start + OUT_STEP] = product[rows:]


def lane_sums(values):
    total = values[:, :HEAD_DIM]
    for start in range(HEAD_DIM, values.shape[1], HEAD_DIM):
        total = total + values[:, start : start + HEAD_DIM]
    return total


def norm_kernel(near_ref, far_ref, residual_ref, gain_ref, unit_ref, sigma_ref, normed_ref):
    rows, width = residual_ref.shape
    spans = [slice(at, at + NORM_STEP) for at in range(0, width, NORM_STEP)]
    total = jnp.zeros((rows, HEAD_DIM), F32)
    for cols in spans:
        stream = residual_ref[:, cols].astype(F32) + near_ref[:, cols].astype(F32) + far_ref[:, cols].astype(F32)
        unit_ref[:, cols] = stream
        total = total + lane_sums(stream)
    mean = jnp.sum(total, axis=-1, keepdims=True) / width
    total = jnp.zeros((rows, HEAD_DIM), F32)
    for cols in spans:
        centered = unit_ref[:, cols] - mean
        total = total + lane_sums(centered * centered)
    sigma = jnp.sqrt(jnp.sum(total, axis=-1, keepdims=True) / width + EPSILON)
    sigma_ref[...] = jnp.broadcast_to(sigma, sigma_ref.shape)
    inverse = 1.0 / sigma
    for cols in spans:
        unit = (unit_ref[:, cols] - mean) * inverse
        unit_ref[:, cols] = unit
        normed_ref[:, cols] = (unit * gain_ref[:, cols]).astype(BF16)


def norm_back_kernel(near_ref, far_ref, cot_ref, gain_ref, unit_ref, sigma_ref, low_ref, scaled_ref):
    rows, width = cot_ref.shape
    spans = [slice(at, at + NORM_STEP) for at in range(0, width, NORM_STEP)]
    total = jnp.zeros((rows, HEAD_DIM), F32)
    total_along = jnp.zeros((rows, HEAD_DIM), F32)
    for cols in spans:
        grad = cot_ref[:, cols].astype(F32) + near_ref[:, cols].astype(F32) + far_ref[:, cols].astype(F32)
        scaled = grad * gain_ref[:, cols]
        scaled_ref[:, cols] = scaled
        total = total + lane_sums(scaled)
        total_along = total_along + lane_sums(scaled * unit_ref[:, cols])
    mean = jnp.sum(total, axis=-1, keepdims=True) / width
    along = jnp.sum(total_along, axis=-1, keepdims=True) / width
    inverse = 1.0 / sigma_ref[:, :1]
    for cols in spans:
        grad = (scaled_ref[:, cols] - mean - unit_ref[:, cols] * along) * inverse
        low_ref[:, cols] = grad.astype(BF16)


def gelu_and_slope(v):
    root = math.sqrt(2.0 / math.pi)
    square = v * v
    t = jnp.tanh(v * (root + root * 0.044715 * square))
    plus = 0.5 + 0.5 * t
    slope = plus + 0.5 * v * (1.0 - t * t) * (root + 3.0 * root * 0.044715 * square)
    return v * plus, slope


def ffn_kernel(
    own_ref, near_ref, up_ref, pick_ref, grad_ref, grad_copy_ref, inverse_ref, gain_ref, merged_ref, hidden_grad_ref
):
    rows = jnp.concatenate([own_ref[...], near_ref[...]], axis=0)
    source = dot(rows, up_ref[...])
    high = source.astype(BF16)
    low = (source - high.astype(F32)).astype(BF16)
    copied = (dot(high, pick_ref[...]) + dot(low, pick_ref[...])) * gain_ref[...]
    act_copy, slope_copy = gelu_and_slope(copied)
    act, slope = gelu_and_slope(source)
    back_copy = (grad_copy_ref[...] * slope_copy).astype(BF16)
    hidden_grad_ref[...] = (grad_ref[...] * slope + dot_nt(back_copy, pick_ref[...])).astype(BF16)
    merged = act + dot_nt(act_copy.astype(BF16), pick_ref[...])
    merged_ref[...] = (merged * inverse_ref[...]).astype(BF16)


def back_kernel(hidden_grad_ref, up_ref, own_ref, other_ref):
    rows, width = own_ref.shape
    for start in range(0, width, OUT_STEP):
        product = dot_nt(hidden_grad_ref[...], up_ref[start : start + OUT_STEP]).astype(BF16)
        own_ref[:, start : start + OUT_STEP] = product[:rows]
        other_ref[:, start : start + OUT_STEP] = product[rows:]


def grad_attended_own_kernel(low_ref, weight_ref, grad_ref):
    grad_ref[...] = dot_nt(low_ref[...], weight_ref[...]).astype(BF16)


def grad_attended_kernel(own_ref, near_ref, weight_ref, att_ref, pack_ref, delta_ref):
    rows, width = att_ref.shape
    heads = width // HEAD_DIM
    pack_ref[: rows // 2] = own_ref[...]
    pack_ref[rows // 2 : rows] = dot_nt(near_ref[...], weight_ref[...]).astype(BF16)
    product = pack_ref[:rows].astype(F32) * att_ref[...].astype(F32)
    lane = lax.broadcasted_iota(jnp.int32, (rows, HEAD_DIM), 1)
    delta = jnp.zeros((rows, HEAD_DIM), F32)
    for head in range(heads):
        part = jnp.sum(product[:, head * HEAD_DIM : (head + 1) * HEAD_DIM], axis=1, keepdims=True)
        delta = jnp.where(lane == head, part, delta)
    delta_ref[...] = delta
    pack_ref[rows:, :rows] = stat_rows(delta, heads)
    pack_ref[rows:, rows:] = jnp.zeros((STAT_ROWS, width - rows), BF16)


def grad_query_kernel(scale, place, q_pack, do_pack, lse_ref, delta_ref, *refs):
    key_refs, value_refs, grad_ref = refs[0:10:2], refs[1:10:2], refs[10]
    rows, width = grad_ref.shape
    heads = width // HEAD_DIM
    slab = rows // 4
    seq, blocks, core = place[0], place[1], place[2]

    @pl.loop(0, heads)
    def _(head):
        cols = head_columns(head)
        query, out_grad = q_pack[:rows, cols], do_pack[:rows, cols]
        lse, delta = pick_lane(lse_ref[...], head), pick_lane(delta_ref[...], head)
        total = jnp.zeros((rows, HEAD_DIM), F32)
        for index, offset in enumerate((0,) + nearby_offsets(seq)):
            key, value = key_refs[index][:, cols], value_refs[index][:, cols]
            score = dot_nt(query, key) * (scale * LOG2E) - lse
            if index > 0:
                valid = (seq + offset >= 0) & (seq + offset < blocks)
                score = jnp.where(valid, score, -1e30)
            grad_score = jnp.exp2(score) * (dot_nt(out_grad, value) - delta)
            total = total + dot(grad_score.astype(BF16), key)
        total = total * scale
        for index, start in enumerate(local_starts(core, rows)):
            grad_ref[pl.ds(start, slab), cols] = total[index * slab : (index + 1) * slab]


def grad_key_value_kernel(scale, count, start, *refs):
    packs, refs = refs[: 2 * count], refs[2 * count :]
    k0, v0 = refs[:2]
    grad_key_ref, grad_value_ref = refs[-2:]
    rows, width = k0.shape
    heads = width // HEAD_DIM

    for head in range(heads):
        cols = slice(head * HEAD_DIM, (head + 1) * HEAD_DIM)
        key, value = k0[:, cols], v0[:, cols]
        grad_key = jnp.zeros((rows, HEAD_DIM), F32)
        grad_value = jnp.zeros((rows, HEAD_DIM), F32)
        for index in range(count):
            q_pack, do_pack = packs[2 * index], packs[2 * index + 1]
            query, out_grad = q_pack[:rows, cols], do_pack[:rows, cols]
            score = dot_nt(key, query) * (scale * LOG2E) - read_stat(q_pack, head, heads, rows)
            weight = jnp.exp2(score)
            grad_value = grad_value + dot(weight.astype(BF16), out_grad)
            grad_score = weight * (dot_nt(value, out_grad) - read_stat(do_pack, head, heads, rows))
            grad_key = grad_key + dot(grad_score.astype(BF16), query)
        grad_key = grad_key * scale
        if not start:
            grad_key = grad_key + refs[2][:, cols]
            grad_value = grad_value + refs[3][:, cols]
        grad_key_ref[:, cols] = grad_key
        grad_value_ref[:, cols] = grad_value


def shards(
    query_heads,
    key_heads,
    value_heads,
    residual,
    out_weight,
    ln_gain,
    up_source,
    down_source,
    copy_gain,
    neuron_source,
    cotangent,
):
    rows, head_width = query_heads.shape
    model_width = residual.shape[1]
    src_width = up_source.shape[1]
    half = rows // 2
    scale = 1.0 / math.sqrt(HEAD_DIM)
    seq = lax.axis_index("seq")
    blocks = lax.axis_size("seq")
    tp_place = lax.axis_index("tp")
    core, chip = tp_place % 2, tp_place // 2
    place = jnp.stack([seq, jnp.full_like(seq, blocks), core]).astype(jnp.int32)

    window = [key_heads, value_heads]
    first = [(swap_block(array, 1), swap_block(array, 0)) for array in (key_heads, value_heads)]
    second = [(swap_block(b, 1), swap_block(a, 0)) for a, b in first]
    for (keys, values) in zip(first[0] + second[0], first[1] + second[1]):
        window += [keys, values]

    attended, q_pack, lse = call(
        functools.partial(attention_kernel, scale),
        (
            shape((rows, head_width), BF16),
            shape((rows + STAT_ROWS, head_width), BF16),
            shape((rows, HEAD_DIM), F32),
        ),
        [SMEM] + [VMEM] * 11,
    )(place, query_heads, *window)

    def two_parts(kernel, operands):
        return call(kernel, (shape((half, model_width), BF16),) * 2, [VMEM, VMEM])(*operands)

    def chip_sum(own, other):
        return own.astype(F32) + swap_core(other).astype(F32)

    near = chip_sum(*two_parts(out_kernel, (attended, out_weight))).astype(BF16)
    far = swap_chip(near)

    def half_rows(array, place):
        split = array.reshape(2, 2, half // 2, array.shape[1])
        return lax.dynamic_slice_in_dim(split, place, 1, 1).reshape(half, array.shape[1])

    cot_own = half_rows(cotangent, core)
    cot_local = jnp.concatenate([cot_own, half_rows(cotangent, 1 - core)], axis=0)
    grad_merged = dot_nt(after(cot_local, near), down_source)

    residual_own = half_rows(residual, core)
    local_source = neuron_source - tp_place * src_width
    pick = (lax.broadcasted_iota(jnp.int32, (src_width, src_width), 0) == local_source[None, :])
    counts = 1.0 + jnp.sum(pick.astype(F32), axis=1)
    pick = pick.astype(BF16)
    inverse = 1.0 / counts
    grad_merged = grad_merged * inverse
    grad_high = grad_merged.astype(BF16)
    grad_rest = (grad_merged - grad_high.astype(F32)).astype(BF16)
    grad_copy = (dot(grad_high, pick) + dot(grad_rest, pick)) * copy_gain
    gain_row = ln_gain.reshape(1, model_width)
    inverse_row = inverse.reshape(1, src_width)
    copy_row = copy_gain.reshape(1, src_width)

    far, pick, grad_merged, grad_copy = lax.optimization_barrier((far, pick, grad_merged, grad_copy))

    far, q_a = lax.optimization_barrier((far, swap_block(after(q_pack, near), 0)))

    unit, sigma, normed = call(
        norm_kernel,
        (
            shape((half, model_width), F32),
            shape((half, HEAD_DIM), F32),
            shape((half, model_width), BF16),
        ),
        [VMEM] * 4,
    )(near, far, residual_own, gain_row)
    near_normed = swap_core(normed)
    merged, hidden_grad = call(ffn_kernel, (shape((rows, src_width), BF16),) * 2, [VMEM] * 8)(
        normed, near_normed, up_source, pick, grad_merged, grad_copy, inverse_row, copy_row
    )
    ffn_parts = two_parts(out_kernel, (merged, down_source))
    hidden_grad, ffn_parts, q_b = lax.optimization_barrier(
        (hidden_grad, ffn_parts, swap_block(after(q_pack, normed), 1))
    )
    near = chip_sum(*two_parts(back_kernel, (hidden_grad, up_source))).astype(BF16)
    far = swap_chip(near)
    ffn_chip = chip_sum(*ffn_parts).reshape(2, half // 2, model_width)
    ffn_send = jnp.where(chip == 0, ffn_chip[1], ffn_chip[0]).astype(BF16)
    ffn_mine = jnp.where(chip == 0, ffn_chip[0], ffn_chip[1])
    q_c = swap_block(after(q_b, near), 0)
    far, ffn_send, ffn_mine, q_c = lax.optimization_barrier((far, ffn_send, ffn_mine, q_c))

    low = call(
        norm_back_kernel,
        shape((half, model_width), BF16),
        [VMEM] * 6,
        scratch=[pltpu.VMEM((half, model_width), F32)],
    )(near, far, cot_own, gain_row, unit, sigma)
    near_low = swap_core(low)
    ffn_far = swap_chip(after(ffn_send, low))
    grad_own = call(grad_attended_own_kernel, shape((half, head_width), BF16), [VMEM] * 2)(low, out_weight)
    near_low, grad_own = lax.optimization_barrier((near_low, grad_own))
    do_pack, delta = call(
        grad_attended_kernel,
        (shape((rows + STAT_ROWS, head_width), BF16), shape((rows, HEAD_DIM), F32)),
        [VMEM] * 4,
    )(grad_own, near_low, out_weight, attended)

    do_a, do_b = swap_block(do_pack, 0), swap_block(do_pack, 1)

    q_d = swap_block(after(q_a, do_pack), 1)
    do_a, do_b, do_own = lax.optimization_barrier((do_a, do_b, do_pack))
    do_c, do_d = swap_block(do_b, 0), swap_block(do_a, 1)
    grad_query = call(
        functools.partial(grad_query_kernel, scale),
        shape((rows, head_width), F32),
        [SMEM] + [VMEM] * 14,
    )(place, q_pack, do_own, lse, delta, *window)

    def grad_key_value(pairs, sums):
        return call(
            functools.partial(grad_key_value_kernel, scale, len(pairs), not sums),
            (shape((rows, head_width), F32),) * 2,
            [VMEM] * (2 * len(pairs) + 2 + len(sums)),
        )(*[pack for pair in pairs for pack in pair], key_heads, value_heads, *sums)

    sums = grad_key_value([(q_pack, do_own), (q_a, do_a), (q_b, do_b)], ())
    own_unit = lax.dynamic_slice_in_dim(unit, chip * (half // 2), half // 2, 0)
    encoded = own_unit * ln_gain + (ffn_mine + after(ffn_far, grad_query, *sums).astype(F32))
    grad_key, grad_value = grad_key_value([(q_c, do_c), (q_d, do_d)], sums)

    col_width = model_width // lax.axis_size("tp")
    first = jnp.where(core == 0, low, near_low).reshape(2, half // 2, model_width)
    second = jnp.where(core == 0, near_low, low).reshape(2, half // 2, model_width)
    low_all = jnp.stack([first, second], axis=1).reshape(rows, model_width)
    grad_residual = lax.dynamic_slice_in_dim(low_all, tp_place * col_width, col_width, 1).astype(F32)
    return (encoded, grad_query, grad_key, grad_value, grad_residual)


def solution(mesh):
    in_specs = (
        P("seq", "tp"),
        P("seq", "tp"),
        P("seq", "tp"),
        P("seq", None),
        P("tp", None),
        P(),
        P(None, "tp"),
        P("tp", None),
        P("tp"),
        P("tp"),
        P("seq", None),
    )
    out_specs = (
        P(("seq", "tp"), None),
        P("seq", "tp"),
        P("seq", "tp"),
        P("seq", "tp"),
        P("seq", "tp"),
    )
    return jax.shard_map(shards, mesh=mesh, in_specs=in_specs, out_specs=out_specs, check_vma=False)
```

profile of v0, /device:TPU:5, one launch (start us, length us, event | category | flops | bytes accessed | tf_op | source)
XLA Modules:
  0.0 164.7 jit_solution(1930422459129235719)
XLA Ops:
  0.6 1.7 %collective-permute-start.2 = (bf16[256,512]{1,0:T(8,128)(2,1)}, bf16[256,512]{1,0:T(8,128)(2,1)}, u32[]{:S(2)}, u32[]{:S(2)}) collective-permute-start(bf16[256,512]{1,0:T(8,128)(2,1)} %refs_4_.1), channel_id=1, source_target_pairs={{0,4},{8,12},{16,20},{24,28},{32,36},{40,44},{48,52},{56,60},{64,6... | collective-permute-start | bytes 786440 | tf_op jit(solution)/shard_map/ppermute | solution.py:66
  2.4 5.3 %collective-permute-start = (bf16[256,512]{1,0:T(8,128)(2,1)}, bf16[256,512]{1,0:T(8,128)(2,1)}, u32[]{:S(2)}, u32[]{:S(2)}) collective-permute-start(bf16[256,512]{1,0:T(8,128)(2,1)} %refs_4_.1), channel_id=1, source_target_pairs={{4,8},{12,16},{20,24},{28,32},{36,40},{44,48},{52,56},{60,64},{68,... | collective-permute-start | bytes 786440 | tf_op jit(solution)/shard_map/ppermute | solution.py:66
  7.7 3.1 %collective-permute-start.1 = (bf16[256,512]{1,0:T(8,128)(2,1)}, bf16[256,512]{1,0:T(8,128)(2,1)}, u32[]{:S(2)}, u32[]{:S(2)}) collective-permute-start(bf16[256,512]{1,0:T(8,128)(2,1)} %refs_5_.1), channel_id=1, source_target_pairs={{4,8},{12,16},{20,24},{28,32},{36,40},{44,48},{52,56},{60,64},{68,... | collective-permute-start | bytes 786440 | tf_op jit(solution)/shard_map/ppermute | solution.py:66
  11.6 1.0 constant_dynamic-slice_fusion
  13.2 5.5 %collective-permute-start.4 = (bf16[256,512]{1,0:T(8,128)(2,1)}, bf16[256,512]{1,0:T(8,128)(2,1)S(1)}, u32[]{:S(2)}, u32[]{:S(2)}) collective-permute-start(bf16[256,512]{1,0:T(8,128)(2,1)} %collective-permute-done.2.refs_4_), channel_id=1, source_target_pairs={{4,8},{12,16},{20,24},{28,32},{36,40},{44,48},{52,56},{60,64},{68,... | collective-permute-start | bytes 786440 | tf_op jit(solution)/shard_map/ppermute | solution.py:66
  18.8 3.1 %collective-permute-start.5 = (bf16[256,512]{1,0:T(8,128)(2,1)}, bf16[256,512]{1,0:T(8,128)(2,1)S(1)}, u32[]{:S(2)}, u32[]{:S(2)}) collective-permute-start(bf16[256,512]{1,0:T(8,128)(2,1)} %collective-permute-done.3.refs_5_), channel_id=1, source_target_pairs={{4,8},{12,16},{20,24},{28,32},{36,40},{44,48},{52,56},{60,64},{68,... | collective-permute-start | bytes 786440 | tf_op jit(solution)/shard_map/ppermute | solution.py:66
  23.1 2.0 %collective-permute-done.4.refs_6_ = bf16[256,512]{1,0:T(8,128)(2,1)S(1)} collective-permute-done((bf16[256,512]{1,0:T(8,128)(2,1)}, bf16[256,512]{1,0:T(8,128)(2,1)S(1)}, u32[]{:S(2)}, u32[]{:S(2)}) %collective-permute-start.4) | collective-permute-done | bytes 262176 | tf_op jit(solution)/shard_map/ppermute | solution.py:66
  25.1 5.6 %collective-permute-done.5.refs_7_ = bf16[256,512]{1,0:T(8,128)(2,1)S(1)} collective-permute-done((bf16[256,512]{1,0:T(8,128)(2,1)}, bf16[256,512]{1,0:T(8,128)(2,1)S(1)}, u32[]{:S(2)}, u32[]{:S(2)}) %collective-permute-start.5) | collective-permute-done | bytes 262176 | tf_op jit(solution)/shard_map/ppermute | solution.py:66
  30.8 4.0 %shard_map.146 = (bf16[256,512]{1,0:T(8,128)(2,1)S(1)}, bf16[272,512]{1,0:T(8,128)(2,1)S(1)}, f32[256,128]{1,0:T(8,128)S(1)}) custom-call(s32[3]{0:T(128)S(1)} %pad_add_fusion.place, bf16[256,512]{1,0:T(8,128)(2,1)S(1)} %copy-done.35, bf16[256,512]{1,0:T(8,128)(2,1)S(1)} %copy-done.9, bf16[256,512]{1,0:T(8,128)(2,1)S(1)} %copy-done.10, ...), custom_call_target="tpu_custom_call" | custom-call | flops 1024 | bytes 1024 | tf_op jit(solution)/shard_map/pallas_call | solution.py:343
  34.8 2.3 %shard_map.147 = (bf16[128,4096]{1,0:T(8,128)(2,1)S(1)}, bf16[128,4096]{1,0:T(8,128)(2,1)}) custom-call(bf16[256,512]{1,0:T(8,128)(2,1)S(1)} %get-tuple-element.51.att_ref, bf16[512,4096]{1,0:T(8,128)(2,1)S(1)} %copy-done.2), custom_call_target="tpu_custom_call" | custom-call | flops 1024 | bytes 1024 | tf_op jit(solution)/shard_map/pallas_call | solution.py:354
  37.1 1.0 copy-done.15
  38.1 2.5 %collective-permute-start.8 = (bf16[128,4096]{1,0:T(8,128)(2,1)}, bf16[128,4096]{1,0:T(8,128)(2,1)}, u32[]{:S(2)}, u32[]{:S(2)}) collective-permute-start(bf16[128,4096]{1,0:T(8,128)(2,1)} %get-tuple-element.53), channel_id=1, source_target_pairs={{0,1},{1,0},{2,3},{3,2},{4,5},{5,4},{6,7},{7,6},{8,9},{9,8},{10,11... | collective-permute-start | bytes 3145736 | tf_op jit(solution)/shard_map/ppermute | solution.py:52
  40.6 1.7 %constant_dynamic-slice_fusion.2 = (bf16[2,1,64,4096]{3,2,1,0:T(8,128)(2,1)S(1)}, bf16[2,1,64,4096]{3,2,1,0:T(8,128)(2,1)S(1)}) fusion(bf16[2,2,64,4096]{3,2,1,0:T(8,128)(2,1)} %bitcast.37, s32[]{:T(128)S(6)} %select_n.49, s32[]{:T(128)S(6)} %select_n.50), kind=kLoop, calls=%fused_computation.28 | loop fusion | bytes 4194312 | tf_op jit(solution)/shard_map/dynamic_slice | solution.py:364
  43.5 1.5 add_convert_fusion.1.near_ref
  45.0 2.8 %collective-permute-start.9 = (bf16[128,4096]{1,0:T(8,128)(2,1)S(1)}, bf16[128,4096]{1,0:T(8,128)(2,1)S(1)}, u32[]{:S(2)}, u32[]{:S(2)}) collective-permute-start(bf16[128,4096]{1,0:T(8,128)(2,1)S(1)} %add_convert_fusion.1.near_ref), channel_id=1, source_target_pairs={{0,2},{2,0},{1,3},{3,1},{4,6},{6,4},{5,7},{7,5},{8,10},{10,8},{9,1... | collective-permute-start | bytes 3145736 | tf_op jit(solution)/shard_map/ppermute | solution.py:56
  47.8 5.9 %convolution_multiply_fusion.grad_ref = f32[256,1024]{1,0:T(8,128)S(1)} fusion(bf16[256,4096]{1,0:T(8,128)(2,1)S(1)} %pad_maximum_fusion, bf16[1024,4096]{1,0:T(8,128)(2,1)} %weight_ref.5, f32[1024]{0:T(1024)S(1)} %add_divide_fusion), kind=kOutput, calls=%fused_computation.14 | convolution fusion | flops 2147745792 | bytes 11538432 | tf_op jit(solution)/shard_map/dot_general | solution.py:48
  53.7 1.1 fusion
  54.9 1.8 %fusion.6.grad_copy_ref = f32[256,1024]{1,0:T(8,128)S(1)} fusion(f32[256,1024]{1,0:T(8,128)S(1)} %fusion, s32[1024]{0:T(1024)} %copy-done.46, f32[1024]{0:T(1024)S(1)} %copy-done.43, f32[256,1024]{1,0:T(8,128)S(1)} %convolution_multiply_fusion.grad_ref), kind=kOutput, calls=%fused_computation.13 | convolution fusion | flops 538705920 | bytes 3153920 | tf_op jit(solution)/shard_map/dot_general | solution.py:44
  56.7 14.6 %collective-permute-done.9.far_ref = bf16[128,4096]{1,0:T(8,128)(2,1)S(1)} collective-permute-done((bf16[128,4096]{1,0:T(8,128)(2,1)S(1)}, bf16[128,4096]{1,0:T(8,128)(2,1)S(1)}, u32[]{:S(2)}, u32[]{:S(2)}) %collective-permute-start.9) | collective-permute-done | bytes 1048608 | tf_op jit(solution)/shard_map/ppermute | solution.py:56
  71.4 1.2 shard_map.148
  74.0 5.3 %collective-permute-start.12 = (bf16[272,512]{1,0:T(8,128)(2,1)S(1)}, bf16[272,512]{1,0:T(8,128)(2,1)S(1)}, u32[]{:S(2)}, u32[]{:S(2)}) collective-permute-start(bf16[272,512]{1,0:T(8,128)(2,1)S(1)} %copy-done.13), channel_id=1, source_target_pairs={{4,8},{12,16},{20,24},{28,32},{36,40},{44,48},{52,56},{60,64},{68,... | collective-permute-start | bytes 835592 | tf_op jit(solution)/shard_map/ppermute | solution.py:66
  79.4 4.7 %shard_map.149 = (bf16[256,1024]{1,0:T(8,128)(2,1)S(1)}, bf16[256,1024]{1,0:T(8,128)(2,1)S(1)}) custom-call(bf16[128,4096]{1,0:T(8,128)(2,1)S(1)} %get-tuple-element.60.own_ref, bf16[128,4096]{1,0:T(8,128)(2,1)S(1)} %collective-permute-done.11.near_ref, bf16[4096,1024]{1,0:T(8,128)(2,1)S(1)} %bitcast.23, bf16[1024,1024]{1,0:T(8,128)(2,1)S(1)} %fusion.2.pick_ref, ...), custom_call_target="tpu_custom_call" | custom-call | flops 1024 | bytes 1024 | tf_op jit(solution)/shard_map/pallas_call | solution.py:398
  84.2 3.3 %shard_map.150 = (bf16[128,4096]{1,0:T(8,128)(2,1)S(1)}, bf16[128,4096]{1,0:T(8,128)(2,1)}) custom-call(bf16[256,1024]{1,0:T(8,128)(2,1)S(1)} %get-tuple-element.65.att_ref, bf16[1024,4096]{1,0:T(8,128)(2,1)S(1)} %bitcast.27), custom_call_target="tpu_custom_call" | custom-call | flops 1024 | bytes 1024 | tf_op jit(solution)/shard_map/pallas_call | solution.py:354
  87.5 1.0 copy-done.27
  88.4 2.4 %shard_map.151 = (bf16[128,4096]{1,0:T(8,128)(2,1)S(1)}, bf16[128,4096]{1,0:T(8,128)(2,1)S(1)}) custom-call(bf16[256,1024]{1,0:T(8,128)(2,1)S(1)} %get-tuple-element.69.hidden_grad_ref, bf16[4096,1024]{1,0:T(8,128)(2,1)S(1)} %bitcast.23), custom_call_target="tpu_custom_call" | custom-call | flops 1024 | bytes 1024 | tf_op jit(solution)/shard_map/pallas_call | solution.py:354
  91.4 2.3 %collective-permute-done.13 = bf16[128,4096]{1,0:T(8,128)(2,1)} collective-permute-done((bf16[128,4096]{1,0:T(8,128)(2,1)S(1)}, bf16[128,4096]{1,0:T(8,128)(2,1)}, u32[]{:S(2)}, u32[]{:S(2)}) %collective-permute-start.13) | collective-permute-done | bytes 1048608 | tf_op jit(solution)/shard_map/ppermute | solution.py:52
  93.7 1.5 add_convert_fusion.near_ref
  95.2 2.7 %collective-permute-start.14 = (bf16[128,4096]{1,0:T(8,128)(2,1)S(1)}, bf16[128,4096]{1,0:T(8,128)(2,1)S(1)}, u32[]{:S(2)}, u32[]{:S(2)}) collective-permute-start(bf16[128,4096]{1,0:T(8,128)(2,1)S(1)} %add_convert_fusion.near_ref), channel_id=1, source_target_pairs={{0,2},{2,0},{1,3},{3,1},{4,6},{6,4},{5,7},{7,5},{8,10},{10,8},{9,1... | collective-permute-start | bytes 3145736 | tf_op jit(solution)/shard_map/ppermute | solution.py:56
  97.9 1.8 %convert_add_fusion = f32[128,4096]{1,0:T(8,128)S(1)} fusion(bf16[128,4096]{1,0:T(8,128)(2,1)} %collective-permute-done.15, bf16[128,4096]{1,0:T(8,128)(2,1)} %copy-done.27), kind=kLoop, calls=%fused_computation.7 | loop fusion | flops 1572864 | bytes 4194304 | tf_op jit(solution)/shard_map/add | solution.py:357
  99.7 1.1 slice_select_fusion
  101.7 3.9 %collective-permute-done.16.refs_0_ = bf16[272,512]{1,0:T(8,128)(2,1)S(1)} collective-permute-done((bf16[272,512]{1,0:T(8,128)(2,1)S(1)}, bf16[272,512]{1,0:T(8,128)(2,1)S(1)}, u32[]{:S(2)}, u32[]{:S(2)}) %collective-permute-start.16) | collective-permute-done | bytes 278560 | tf_op jit(solution)/shard_map/ppermute | solution.py:66
  106.3 15.0 %collective-permute-done.14.far_ref = bf16[128,4096]{1,0:T(8,128)(2,1)S(1)} collective-permute-done((bf16[128,4096]{1,0:T(8,128)(2,1)S(1)}, bf16[128,4096]{1,0:T(8,128)(2,1)S(1)}, u32[]{:S(2)}, u32[]{:S(2)}) %collective-permute-start.14) | collective-permute-done | bytes 1048608 | tf_op jit(solution)/shard_map/ppermute | solution.py:56
  121.3 1.3 shard_map.152.low_ref
  122.6 1.1 collective-permute-start.18
  123.7 2.2 %copy-done.3 = bf16[512,4096]{1,0:T(8,128)(2,1)S(1)} copy-done((bf16[512,4096]{1,0:T(8,128)(2,1)S(1)}, bf16[512,4096]{1,0:T(8,128)(2,1)}, u32[]{:S(2)}) %copy-start.3) | copy-done | bytes 4194328
  125.9 1.5 shard_map.153.own_ref
  127.5 3.0 %collective-permute-start.17 = (bf16[64,4096]{1,0:T(8,128)(2,1)S(1)}, bf16[64,4096]{1,0:T(8,128)(2,1)S(1)}, u32[]{:S(2)}, u32[]{:S(2)}) collective-permute-start(bf16[64,4096]{1,0:T(8,128)(2,1)S(1)} %copy-done.45), channel_id=1, source_target_pairs={{0,2},{2,0},{1,3},{3,1},{4,6},{6,4},{5,7},{7,5},{8,10},{10,8},{9,1... | collective-permute-start | bytes 1572872 | tf_op jit(solution)/shard_map/ppermute | solution.py:56
  130.4 1.7 %shard_map.154 = (bf16[272,512]{1,0:T(8,128)(2,1)S(1)}, f32[256,128]{1,0:T(8,128)S(1)}) custom-call(bf16[128,512]{1,0:T(8,128)(2,1)S(1)} %shard_map.153.own_ref, bf16[128,4096]{1,0:T(8,128)(2,1)S(1)} %collective-permute-done.18.near_ref, bf16[512,4096]{1,0:T(8,128)(2,1)S(1)} %copy-done.4, bf16[256,512]{1,0:T(8,128)(2,1)S(1)} %copy-done.26), custom_call_target="tpu_custom_call" | custom-call | flops 1024 | bytes 1024 | tf_op jit(solution)/shard_map/pallas_call | solution.py:423
  132.1 4.2 %collective-permute-start.20 = (bf16[272,512]{1,0:T(8,128)(2,1)S(1)}, bf16[272,512]{1,0:T(8,128)(2,1)S(1)}, u32[]{:S(2)}, u32[]{:S(2)}) collective-permute-start(bf16[272,512]{1,0:T(8,128)(2,1)S(1)} %get-tuple-element.84.do_pack.refs_1_), channel_id=1, source_target_pairs={{4,8},{12,16},{20,24},{28,32},{36,40},{44,48},{52,56},{60,64},{68,... | collective-permute-start | bytes 835592 | tf_op jit(solution)/shard_map/ppermute | solution.py:66
  137.7 4.2 %collective-permute-start.22 = (bf16[272,512]{1,0:T(8,128)(2,1)S(1)}, bf16[272,512]{1,0:T(8,128)(2,1)S(1)}, u32[]{:S(2)}, u32[]{:S(2)}) collective-permute-start(bf16[272,512]{1,0:T(8,128)(2,1)S(1)} %copy-done.29), channel_id=1, source_target_pairs={{4,8},{12,16},{20,24},{28,32},{36,40},{44,48},{52,56},{60,64},{68,... | collective-permute-start | bytes 835592 | tf_op jit(solution)/shard_map/ppermute | solution.py:66
  142.0 1.1 dynamic-slice_convert_fusion
  143.1 1.9 %collective-permute-done.20.refs_5_ = bf16[272,512]{1,0:T(8,128)(2,1)S(1)} collective-permute-done((bf16[272,512]{1,0:T(8,128)(2,1)S(1)}, bf16[272,512]{1,0:T(8,128)(2,1)S(1)}, u32[]{:S(2)}, u32[]{:S(2)}) %collective-permute-start.20) | collective-permute-done | bytes 278560 | tf_op jit(solution)/shard_map/ppermute | solution.py:66
  145.0 4.2 %collective-permute-start.23 = (bf16[272,512]{1,0:T(8,128)(2,1)S(1)}, bf16[272,512]{1,0:T(8,128)(2,1)S(1)}, u32[]{:S(2)}, u32[]{:S(2)}) collective-permute-start(bf16[272,512]{1,0:T(8,128)(2,1)S(1)} %collective-permute-done.19.refs_3_), channel_id=1, source_target_pairs={{4,8},{12,16},{20,24},{28,32},{36,40},{44,48},{52,56},{60,64},{68,... | collective-permute-start | bytes 835592 | tf_op jit(solution)/shard_map/ppermute | solution.py:66
  149.3 2.7 %shard_map.156 = (f32[256,512]{1,0:T(8,128)S(1)}, f32[256,512]{1,0:T(8,128)S(1)}) custom-call(bf16[272,512]{1,0:T(8,128)(2,1)S(1)} %copy-done.14, bf16[272,512]{1,0:T(8,128)(2,1)S(1)} %get-tuple-element.84.do_pack.refs_1_, bf16[272,512]{1,0:T(8,128)(2,1)S(1)} %copy-done.29, bf16[272,512]{1,0:T(8,128)(2,1)S(1)} %collective-permute-done.19.refs_3_, ...), custom_call_target="tpu_custom_call" | custom-call | flops 1024 | bytes 1024 | tf_op jit(solution)/shard_map/pallas_call | solution.py:441
  152.1 6.4 %shard_map.155 = f32[256,512]{1,0:T(8,128)} custom-call(s32[3]{0:T(128)S(1)} %copy-done.42, bf16[272,512]{1,0:T(8,128)(2,1)S(1)} %copy-done.14, bf16[272,512]{1,0:T(8,128)(2,1)S(1)} %get-tuple-element.84.do_pack.refs_1_, f32[256,128]{1,0:T(8,128)S(1)} %get-tuple-element.85.lse_ref, f32[256,128]{1,0:T(8,128)S(1)} %get-tuple-element.86.delta_ref, ...), custom_call_target="tpu_custom_call" | custom-call | flops 1024 | bytes 1024 | tf_op jit(solution)/shard_map/pallas_call | solution.py:434
  158.5 2.3 %collective-permute-done.17 = bf16[64,4096]{1,0:T(8,128)(2,1)S(1)} collective-permute-done((bf16[64,4096]{1,0:T(8,128)(2,1)S(1)}, bf16[64,4096]{1,0:T(8,128)(2,1)S(1)}, u32[]{:S(2)}, u32[]{:S(2)}) %collective-permute-start.17) | collective-permute-done | bytes 524320 | tf_op jit(solution)/shard_map/ppermute | solution.py:56
  160.8 1.1 add_add_fusion
  161.9 2.8 %shard_map.157 = (f32[256,512]{1,0:T(8,128)}, f32[256,512]{1,0:T(8,128)}) custom-call(bf16[272,512]{1,0:T(8,128)(2,1)S(1)} %copy-done.34, bf16[272,512]{1,0:T(8,128)(2,1)S(1)} %collective-permute-done.21.refs_1_, bf16[272,512]{1,0:T(8,128)(2,1)S(1)} %collective-permute-done.22.refs_2_, bf16[272,512]{1,0:T(8,128)(2,1)S(1)} %collective-permute-done.23.refs_3_, ...), custom_call_target="tpu_custom_call" | custom-call | flops 1024 | bytes 1024 | tf_op jit(solution)/shard_map/pallas_call | solution.py:441
  (137 shorter events, 9.2 us)
Async XLA Ops:
  0.6 10.9 %copy-start = (bf16[256,4096]{1,0:T(8,128)(2,1)S(1)}, bf16[256,4096]{1,0:T(8,128)(2,1)}, u32[]{:S(2)}) copy-start(bf16[256,4096]{1,0:T(8,128)(2,1)} %param.14) | copy-start | bytes 6291460
  0.6 12.6 %collective-permute-start.2 = (bf16[256,512]{1,0:T(8,128)(2,1)}, bf16[256,512]{1,0:T(8,128)(2,1)}, u32[]{:S(2)}, u32[]{:S(2)}) collective-permute-start(bf16[256,512]{1,0:T(8,128)(2,1)} %refs_4_.1), channel_id=1, source_target_pairs={{0,4},{8,12},{16,20},{24,28},{32,36},{40,44},{48,52},{56,60},{64,6... | collective-permute-start | bytes 786440 | tf_op jit(solution)/shard_map/ppermute | solution.py:66
  2.4 16.3 %collective-permute-start = (bf16[256,512]{1,0:T(8,128)(2,1)}, bf16[256,512]{1,0:T(8,128)(2,1)}, u32[]{:S(2)}, u32[]{:S(2)}) collective-permute-start(bf16[256,512]{1,0:T(8,128)(2,1)} %refs_4_.1), channel_id=1, source_target_pairs={{4,8},{12,16},{20,24},{28,32},{36,40},{44,48},{52,56},{60,64},{68,... | collective-permute-start | bytes 786440 | tf_op jit(solution)/shard_map/ppermute | solution.py:66
  7.6 11.2 %collective-permute-start.3 = (bf16[256,512]{1,0:T(8,128)(2,1)}, bf16[256,512]{1,0:T(8,128)(2,1)}, u32[]{:S(2)}, u32[]{:S(2)}) collective-permute-start(bf16[256,512]{1,0:T(8,128)(2,1)} %refs_5_.1), channel_id=1, source_target_pairs={{0,4},{8,12},{16,20},{24,28},{32,36},{40,44},{48,52},{56,60},{64,6... | collective-permute-start | bytes 786440 | tf_op jit(solution)/shard_map/ppermute | solution.py:66
  7.7 14.2 %collective-permute-start.1 = (bf16[256,512]{1,0:T(8,128)(2,1)}, bf16[256,512]{1,0:T(8,128)(2,1)}, u32[]{:S(2)}, u32[]{:S(2)}) collective-permute-start(bf16[256,512]{1,0:T(8,128)(2,1)} %refs_5_.1), channel_id=1, source_target_pairs={{4,8},{12,16},{20,24},{28,32},{36,40},{44,48},{52,56},{60,64},{68,... | collective-permute-start | bytes 786440 | tf_op jit(solution)/shard_map/ppermute | solution.py:66
  11.6 42.2 %copy-start.46 = (s32[1024]{0:T(1024)}, s32[1024]{0:T(1024)S(1)}, u32[]{:S(2)}) copy-start(s32[1024]{0:T(1024)S(1)} %broadcast_subtract_fusion) | copy-start | bytes 12292
  11.6 19.2 %copy-start.9 = (bf16[256,512]{1,0:T(8,128)(2,1)S(1)}, bf16[256,512]{1,0:T(8,128)(2,1)}, u32[]{:S(2)}) copy-start(bf16[256,512]{1,0:T(8,128)(2,1)} %refs_4_.1) | copy-start | bytes 786436
  11.6 19.2 %copy-start.10 = (bf16[256,512]{1,0:T(8,128)(2,1)S(1)}, bf16[256,512]{1,0:T(8,128)(2,1)}, u32[]{:S(2)}) copy-start(bf16[256,512]{1,0:T(8,128)(2,1)} %refs_5_.1) | copy-start | bytes 786436
  11.6 19.2 %copy-start.35 = (bf16[256,512]{1,0:T(8,128)(2,1)S(1)}, bf16[256,512]{1,0:T(8,128)(2,1)}, u32[]{:S(2)}) copy-start(bf16[256,512]{1,0:T(8,128)(2,1)} %q_ref.1) | copy-start | bytes 786436
  12.7 22.0 %copy-start.41 = (s32[3]{0:T(128)}, s32[3]{0:T(128)S(1)}, u32[]{:S(2)}) copy-start(s32[3]{0:T(128)S(1)} %pad_add_fusion.place) | copy-start | bytes 40
  13.2 21.6 %copy-start.2 = (bf16[512,4096]{1,0:T(8,128)(2,1)S(1)}, bf16[512,4096]{1,0:T(8,128)(2,1)}, u32[]{:S(2)}) copy-start(bf16[512,4096]{1,0:T(8,128)(2,1)} %weight_ref.7) | copy-start | bytes 12582916
  13.2 11.9 %collective-permute-start.4 = (bf16[256,512]{1,0:T(8,128)(2,1)}, bf16[256,512]{1,0:T(8,128)(2,1)S(1)}, u32[]{:S(2)}, u32[]{:S(2)}) collective-permute-start(bf16[256,512]{1,0:T(8,128)(2,1)} %collective-permute-done.2.refs_4_), channel_id=1, source_target_pairs={{4,8},{12,16},{20,24},{28,32},{36,40},{44,48},{52,56},{60,64},{68,... | collective-permute-start | bytes 786440 | tf_op jit(solution)/shard_map/ppermute | solution.py:66
  18.7 6.4 %collective-permute-start.6 = (bf16[256,512]{1,0:T(8,128)(2,1)}, bf16[256,512]{1,0:T(8,128)(2,1)S(1)}, u32[]{:S(2)}, u32[]{:S(2)}) collective-permute-start(bf16[256,512]{1,0:T(8,128)(2,1)} %collective-permute-done.refs_2_), channel_id=1, source_target_pairs={{0,4},{8,12},{16,20},{24,28},{32,36},{40,44},{48,52},{56,60},{64,6... | collective-permute-start | bytes 786440 | tf_op jit(solution)/shard_map/ppermute | solution.py:66
  18.8 11.9 %collective-permute-start.5 = (bf16[256,512]{1,0:T(8,128)(2,1)}, bf16[256,512]{1,0:T(8,128)(2,1)S(1)}, u32[]{:S(2)}, u32[]{:S(2)}) collective-permute-start(bf16[256,512]{1,0:T(8,128)(2,1)} %collective-permute-done.3.refs_5_), channel_id=1, source_target_pairs={{4,8},{12,16},{20,24},{28,32},{36,40},{44,48},{52,56},{60,64},{68,... | collective-permute-start | bytes 786440 | tf_op jit(solution)/shard_map/ppermute | solution.py:66
  21.9 8.8 %collective-permute-start.7 = (bf16[256,512]{1,0:T(8,128)(2,1)}, bf16[256,512]{1,0:T(8,128)(2,1)S(1)}, u32[]{:S(2)}, u32[]{:S(2)}) collective-permute-start(bf16[256,512]{1,0:T(8,128)(2,1)} %collective-permute-done.1.refs_3_), channel_id=1, source_target_pairs={{0,4},{8,12},{16,20},{24,28},{32,36},{40,44},{48,52},{56,60},{64,6... | collective-permute-start | bytes 786440 | tf_op jit(solution)/shard_map/ppermute | solution.py:66
  38.1 5.1 %collective-permute-start.8 = (bf16[128,4096]{1,0:T(8,128)(2,1)}, bf16[128,4096]{1,0:T(8,128)(2,1)}, u32[]{:S(2)}, u32[]{:S(2)}) collective-permute-start(bf16[128,4096]{1,0:T(8,128)(2,1)} %get-tuple-element.53), channel_id=1, source_target_pairs={{0,1},{1,0},{2,3},{3,2},{4,5},{5,4},{6,7},{7,6},{8,9},{9,8},{10,11... | collective-permute-start | bytes 3145736 | tf_op jit(solution)/shard_map/ppermute | solution.py:52
  45.0 26.3 %collective-permute-start.9 = (bf16[128,4096]{1,0:T(8,128)(2,1)S(1)}, bf16[128,4096]{1,0:T(8,128)(2,1)S(1)}, u32[]{:S(2)}, u32[]{:S(2)}) collective-permute-start(bf16[128,4096]{1,0:T(8,128)(2,1)S(1)} %add_convert_fusion.1.near_ref), channel_id=1, source_target_pairs={{0,2},{2,0},{1,3},{3,1},{4,6},{6,4},{5,7},{7,5},{8,10},{10,8},{9,1... | collective-permute-start | bytes 3145736 | tf_op jit(solution)/shard_map/ppermute | solution.py:56
  47.8 31.5 %slice-start = ((s8[8388608]{0:T(1024)(128)(4,1)}), s8[4194304]{0:T(1024)(128)(4,1)S(1)}, s32[]{:S(2)}) async-start(s8[8388608]{0:T(1024)(128)(4,1)} %bitcast.22), calls=%async_computation | async-start | bytes 8388608
  47.8 31.5 %slice-start.1 = ((s8[8388608]{0:T(1024)(128)(4,1)}), s8[4194304]{0:T(1024)(128)(4,1)S(1)}, s32[]{:S(2)}) async-start(s8[8388608]{0:T(1024)(128)(4,1)} %bitcast.22), calls=%async_computation.1 | async-start | bytes 8388608
  47.8 23.5 %collective-permute-start.10 = (bf16[272,512]{1,0:T(8,128)(2,1)S(1)}, bf16[272,512]{1,0:T(8,128)(2,1)S(1)}, u32[]{:S(2)}, u32[]{:S(2)}) collective-permute-start(bf16[272,512]{1,0:T(8,128)(2,1)S(1)} %copy-done.13), channel_id=1, source_target_pairs={{0,4},{8,12},{16,20},{24,28},{32,36},{40,44},{48,52},{56,60},{64,6... | collective-permute-start | bytes 835592 | tf_op jit(solution)/shard_map/ppermute | solution.py:66
  54.9 16.5 %copy-start.8 = (bf16[2,1,64,4096]{3,2,1,0:T(8,128)(2,1)S(1)}, bf16[2,1,64,4096]{3,2,1,0:T(8,128)(2,1)}, u32[]{:S(2)}) copy-start(bf16[2,1,64,4096]{3,2,1,0:T(8,128)(2,1)} %constant_dynamic-slice_fusion) | copy-start | bytes 3145732
  54.9 16.5 %copy-start.36 = (f32[4096]{0:T(1024)S(1)}, f32[4096]{0:T(1024)}, u32[]{:S(2)}) copy-start(f32[4096]{0:T(1024)} %param.16) | copy-start | bytes 49156
  56.7 22.7 %copy-start.40 = (f32[1024]{0:T(1024)S(1)}, f32[1024]{0:T(1024)}, u32[]{:S(2)}) copy-start(f32[1024]{0:T(1024)} %copy-done.39) | copy-start | bytes 12292
  71.3 12.8 %slice-start.2 = ((s8[8388608]{0:T(1024)(128)(4,1)}), s8[4194304]{0:T(1024)(128)(4,1)S(1)}, s32[]{:S(2)}) async-start(s8[8388608]{0:T(1024)(128)(4,1)} %bitcast.26), calls=%async_computation.2 | async-start | bytes 8388608
  73.2 10.9 %copy-start.5 = (f32[128,4096]{1,0:T(8,128)}, f32[128,4096]{1,0:T(8,128)S(1)}, u32[]{:S(2)}) copy-start(f32[128,4096]{1,0:T(8,128)S(1)} %get-tuple-element.59.unit_ref) | copy-start | bytes 6291460
  73.2 6.1 %collective-permute-start.11 = (bf16[128,4096]{1,0:T(8,128)(2,1)S(1)}, bf16[128,4096]{1,0:T(8,128)(2,1)S(1)}, u32[]{:S(2)}, u32[]{:S(2)}) collective-permute-start(bf16[128,4096]{1,0:T(8,128)(2,1)S(1)} %get-tuple-element.60.own_ref), channel_id=1, source_target_pairs={{0,1},{1,0},{2,3},{3,2},{4,5},{5,4},{6,7},{7,6},{8,9},{9,8},{10,11... | collective-permute-start | bytes 3145736 | tf_op jit(solution)/shard_map/ppermute | solution.py:52
  74.0 13.5 %collective-permute-start.12 = (bf16[272,512]{1,0:T(8,128)(2,1)S(1)}, bf16[272,512]{1,0:T(8,128)(2,1)S(1)}, u32[]{:S(2)}, u32[]{:S(2)}) collective-permute-start(bf16[272,512]{1,0:T(8,128)(2,1)S(1)} %copy-done.13), channel_id=1, source_target_pairs={{4,8},{12,16},{20,24},{28,32},{36,40},{44,48},{52,56},{60,64},{68,... | collective-permute-start | bytes 835592 | tf_op jit(solution)/shard_map/ppermute | solution.py:66
  90.8 2.9 %collective-permute-start.13 = (bf16[128,4096]{1,0:T(8,128)(2,1)S(1)}, bf16[128,4096]{1,0:T(8,128)(2,1)}, u32[]{:S(2)}, u32[]{:S(2)}) collective-permute-start(bf16[128,4096]{1,0:T(8,128)(2,1)S(1)} %get-tuple-element.71), channel_id=1, source_target_pairs={{0,1},{1,0},{2,3},{3,2},{4,5},{5,4},{6,7},{7,6},{8,9},{9,8},{10,11... | collective-permute-start | bytes 3145736 | tf_op jit(solution)/shard_map/ppermute | solution.py:52
  91.2 6.7 %collective-permute-start.15 = (bf16[128,4096]{1,0:T(8,128)(2,1)}, bf16[128,4096]{1,0:T(8,128)(2,1)}, u32[]{:S(2)}, u32[]{:S(2)}) collective-permute-start(bf16[128,4096]{1,0:T(8,128)(2,1)} %get-tuple-element.73), channel_id=1, source_target_pairs={{0,1},{1,0},{2,3},{3,2},{4,5},{5,4},{6,7},{7,6},{8,9},{9,8},{10,11... | collective-permute-start | bytes 3145736 | tf_op jit(solution)/shard_map/ppermute | solution.py:52
  95.2 26.1 %collective-permute-start.14 = (bf16[128,4096]{1,0:T(8,128)(2,1)S(1)}, bf16[128,4096]{1,0:T(8,128)(2,1)S(1)}, u32[]{:S(2)}, u32[]{:S(2)}) collective-permute-start(bf16[128,4096]{1,0:T(8,128)(2,1)S(1)} %add_convert_fusion.near_ref), channel_id=1, source_target_pairs={{0,2},{2,0},{1,3},{3,1},{4,6},{6,4},{5,7},{7,5},{8,10},{10,8},{9,1... | collective-permute-start | bytes 3145736 | tf_op jit(solution)/shard_map/ppermute | solution.py:56
  97.9 7.7 %collective-permute-start.16 = (bf16[272,512]{1,0:T(8,128)(2,1)S(1)}, bf16[272,512]{1,0:T(8,128)(2,1)S(1)}, u32[]{:S(2)}, u32[]{:S(2)}) collective-permute-start(bf16[272,512]{1,0:T(8,128)(2,1)S(1)} %copy-done.31), channel_id=1, source_target_pairs={{0,4},{8,12},{16,20},{24,28},{32,36},{40,44},{48,52},{56,60},{64,6... | collective-permute-start | bytes 835592 | tf_op jit(solution)/shard_map/ppermute | solution.py:66
  99.7 21.6 %copy-start.6 = (f32[128,4096]{1,0:T(8,128)S(1)}, f32[128,4096]{1,0:T(8,128)}, u32[]{:S(2)}) copy-start(f32[128,4096]{1,0:T(8,128)} %copy-done.5) | copy-start | bytes 6291460
  99.7 21.6 %copy-start.38 = (f32[128,128]{1,0:T(8,128)S(1)}, f32[128,128]{1,0:T(8,128)}, u32[]{:S(2)}) copy-start(f32[128,128]{1,0:T(8,128)} %copy-done.37) | copy-start | bytes 196612
  122.6 7.8 %collective-permute-start.18 = (bf16[128,4096]{1,0:T(8,128)(2,1)S(1)}, bf16[128,4096]{1,0:T(8,128)(2,1)S(1)}, u32[]{:S(2)}, u32[]{:S(2)}) collective-permute-start(bf16[128,4096]{1,0:T(8,128)(2,1)S(1)} %shard_map.152.low_ref), channel_id=1, source_target_pairs={{0,1},{1,0},{2,3},{3,2},{4,5},{5,4},{6,7},{7,6},{8,9},{9,8},{10,11... | collective-permute-start | bytes 3145736 | tf_op jit(solution)/shard_map/ppermute | solution.py:52
  127.5 33.3 %collective-permute-start.17 = (bf16[64,4096]{1,0:T(8,128)(2,1)S(1)}, bf16[64,4096]{1,0:T(8,128)(2,1)S(1)}, u32[]{:S(2)}, u32[]{:S(2)}) collective-permute-start(bf16[64,4096]{1,0:T(8,128)(2,1)S(1)} %copy-done.45), channel_id=1, source_target_pairs={{0,2},{2,0},{1,3},{3,1},{4,6},{6,4},{5,7},{7,5},{8,10},{10,8},{9,1... | collective-permute-start | bytes 1572872 | tf_op jit(solution)/shard_map/ppermute | solution.py:56
  132.1 12.9 %collective-permute-start.20 = (bf16[272,512]{1,0:T(8,128)(2,1)S(1)}, bf16[272,512]{1,0:T(8,128)(2,1)S(1)}, u32[]{:S(2)}, u32[]{:S(2)}) collective-permute-start(bf16[272,512]{1,0:T(8,128)(2,1)S(1)} %get-tuple-element.84.do_pack.refs_1_), channel_id=1, source_target_pairs={{4,8},{12,16},{20,24},{28,32},{36,40},{44,48},{52,56},{60,64},{68,... | collective-permute-start | bytes 835592 | tf_op jit(solution)/shard_map/ppermute | solution.py:66
  136.3 8.7 %collective-permute-start.19 = (bf16[272,512]{1,0:T(8,128)(2,1)S(1)}, bf16[272,512]{1,0:T(8,128)(2,1)S(1)}, u32[]{:S(2)}, u32[]{:S(2)}) collective-permute-start(bf16[272,512]{1,0:T(8,128)(2,1)S(1)} %get-tuple-element.84.do_pack.refs_1_), channel_id=1, source_target_pairs={{0,4},{8,12},{16,20},{24,28},{32,36},{40,44},{48,52},{56,60},{64,6... | collective-permute-start | bytes 835592 | tf_op jit(solution)/shard_map/ppermute | solution.py:66
  136.8 12.5 %copy-start.11 = (bf16[256,512]{1,0:T(8,128)(2,1)S(1)}, bf16[256,512]{1,0:T(8,128)(2,1)}, u32[]{:S(2)}) copy-start(bf16[256,512]{1,0:T(8,128)(2,1)} %refs_5_.1) | copy-start | bytes 786436
  136.8 12.5 %copy-start.14 = (bf16[272,512]{1,0:T(8,128)(2,1)S(1)}, bf16[272,512]{1,0:T(8,128)(2,1)}, u32[]{:S(2)}) copy-start(bf16[272,512]{1,0:T(8,128)(2,1)} %copy-done.12) | copy-start | bytes 835588
  136.8 12.5 %copy-start.32 = (bf16[272,512]{1,0:T(8,128)(2,1)S(1)}, bf16[272,512]{1,0:T(8,128)(2,1)}, u32[]{:S(2)}) copy-start(bf16[272,512]{1,0:T(8,128)(2,1)} %copy-done.30) | copy-start | bytes 835588
  137.7 14.3 %copy-start.18 = (bf16[256,512]{1,0:T(8,128)(2,1)S(1)}, bf16[256,512]{1,0:T(8,128)(2,1)}, u32[]{:S(2)}) copy-start(bf16[256,512]{1,0:T(8,128)(2,1)} %copy-done.17) | copy-start | bytes 786436
  137.7 14.3 %copy-start.20 = (bf16[256,512]{1,0:T(8,128)(2,1)S(1)}, bf16[256,512]{1,0:T(8,128)(2,1)}, u32[]{:S(2)}) copy-start(bf16[256,512]{1,0:T(8,128)(2,1)} %copy-done.19) | copy-start | bytes 786436
  137.7 14.3 %copy-start.22 = (bf16[256,512]{1,0:T(8,128)(2,1)S(1)}, bf16[256,512]{1,0:T(8,128)(2,1)}, u32[]{:S(2)}) copy-start(bf16[256,512]{1,0:T(8,128)(2,1)} %copy-done.21) | copy-start | bytes 786436
  137.7 14.3 %copy-start.24 = (bf16[256,512]{1,0:T(8,128)(2,1)S(1)}, bf16[256,512]{1,0:T(8,128)(2,1)}, u32[]{:S(2)}) copy-start(bf16[256,512]{1,0:T(8,128)(2,1)} %copy-done.23) | copy-start | bytes 786436
  137.7 14.3 %copy-start.42 = (s32[3]{0:T(128)S(1)}, s32[3]{0:T(128)}, u32[]{:S(2)}) copy-start(s32[3]{0:T(128)} %copy-done.41) | copy-start | bytes 40
  137.7 24.1 %collective-permute-start.22 = (bf16[272,512]{1,0:T(8,128)(2,1)S(1)}, bf16[272,512]{1,0:T(8,128)(2,1)S(1)}, u32[]{:S(2)}, u32[]{:S(2)}) collective-permute-start(bf16[272,512]{1,0:T(8,128)(2,1)S(1)} %copy-done.29), channel_id=1, source_target_pairs={{4,8},{12,16},{20,24},{28,32},{36,40},{44,48},{52,56},{60,64},{68,... | collective-permute-start | bytes 835592 | tf_op jit(solution)/shard_map/ppermute | solution.py:66
  145.0 16.9 %collective-permute-start.23 = (bf16[272,512]{1,0:T(8,128)(2,1)S(1)}, bf16[272,512]{1,0:T(8,128)(2,1)S(1)}, u32[]{:S(2)}, u32[]{:S(2)}) collective-permute-start(bf16[272,512]{1,0:T(8,128)(2,1)S(1)} %collective-permute-done.19.refs_3_), channel_id=1, source_target_pairs={{4,8},{12,16},{20,24},{28,32},{36,40},{44,48},{52,56},{60,64},{68,... | collective-permute-start | bytes 835592 | tf_op jit(solution)/shard_map/ppermute | solution.py:66
  149.2 12.7 %collective-permute-start.21 = (bf16[272,512]{1,0:T(8,128)(2,1)S(1)}, bf16[272,512]{1,0:T(8,128)(2,1)S(1)}, u32[]{:S(2)}, u32[]{:S(2)}) collective-permute-start(bf16[272,512]{1,0:T(8,128)(2,1)S(1)} %collective-permute-done.20.refs_5_), channel_id=1, source_target_pairs={{0,4},{8,12},{16,20},{24,28},{32,36},{40,44},{48,52},{56,60},{64,6... | collective-permute-start | bytes 835592 | tf_op jit(solution)/shard_map/ppermute | solution.py:66
  (27 other events, 113.6 us)
where the time goes:
time: 167 us; the launch traced here: 165 us
  starting transfers between devices  50.7 us (30%)
  waiting for transfers between devices  48.3 us (29%)
  Pallas kernels  34.1 us (20%)
  other arithmetic  11.6 us (7%)
  local copies, waits for them, and re-layouts  9.69 us (6%)
  matrix products  8.79 us (5%)
    ppermute x16, starting transfers between devices, swap_block(): return lax.ppermute(array, 'seq', ahead + [(j, i) for i, j in ahead])  37.2 us
    ppermute x3, waiting for transfers between devices, swap_chip(): return lax.ppermute(array, 'tp', [(0, 2), (2, 0), (1, 3), (3, 1)])  31.9 us
    ppermute x16, waiting for transfers between devices, swap_block(): return lax.ppermute(array, 'seq', ahead + [(j, i) for i, j in ahead])  13.4 us
    ppermute x3, starting transfers between devices, swap_chip(): return lax.ppermute(array, 'tp', [(0, 2), (2, 0), (1, 3), (3, 1)])  8.48 us
    pallas_call x3, Pallas kernels, two_parts(): call(kernel, (shape((half, model_width), BF16),) * 2, [VMEM, VMEM])  7.94 us
    unnamed x102, local copies, waits for them, and re-layouts  6.71 us
    pallas_call x1, Pallas kernels, shards(): call(functools.partial(grad_query_kernel, scale), shape((rows, head_width...  6.38 us
    dot_general x1, matrix products, dot_nt(): return lax.dot_general(a, b, NT, preferred_element_type=F32)  5.89 us
  transfers between devices with their start and end apart: 24, of which 9 were waited for; matrix products, arithmetic and copies ran while one was open for 13% of the time, Pallas kernels for 12%

commit v1 on v0

--- a/solution.py
+++ b/solution.py
@@ -263,7 +263,7 @@
     slab = rows // 4
     seq, blocks, core = place[0], place[1], place[2]
 
-    @pl.loop(0, heads)
+    @pl.loop(0, heads, unroll=2)
     def _(head):
         cols = head_columns(head)
         query, out_grad = q_pack[:rows, cols], do_pack[:rows, cols]

time: 167 us -> 166 us (level)
  no operation moved by 1% of the time
where the time goes in v1:
time: 166 us; the launch traced here: 165 us
  starting transfers between devices  50.7 us (31%)
  waiting for transfers between devices  48.7 us (29%)
  Pallas kernels  33.7 us (20%)
  other arithmetic  11.6 us (7%)
  local copies, waits for them, and re-layouts  9.69 us (6%)
  matrix products  8.79 us (5%)
    ppermute x16, starting transfers between devices, swap_block(): return lax.ppermute(array, 'seq', ahead + [(j, i) for i, j in ahead])  37.2 us
    ppermute x3, waiting for transfers between devices, swap_chip(): return lax.ppermute(array, 'tp', [(0, 2), (2, 0), (1, 3), (3, 1)])  32.3 us
    ppermute x16, waiting for transfers between devices, swap_block(): return lax.ppermute(array, 'seq', ahead + [(j, i) for i, j in ahead])  13.4 us
    ppermute x3, starting transfers between devices, swap_chip(): return lax.ppermute(array, 'tp', [(0, 2), (2, 0), (1, 3), (3, 1)])  8.48 us
    pallas_call x3, Pallas kernels, two_parts(): call(kernel, (shape((half, model_width), BF16),) * 2, [VMEM, VMEM])  7.94 us
    unnamed x102, local copies, waits for them, and re-layouts  6.71 us
    pallas_call x1, Pallas kernels, shards(): call(functools.partial(grad_query_kernel, scale), shape((rows, head_width...  5.94 us
    dot_general x1, matrix products, dot_nt(): return lax.dot_general(a, b, NT, preferred_element_type=F32)  5.89 us
  transfers between devices with their start and end apart: 24, of which 9 were waited for; matrix products, arithmetic and copies ran while one was open for 13% of the time, Pallas kernels for 12%

profile of v1, /device:TPU:5, one launch (start us, length us, event | category | flops | bytes accessed | tf_op | source)
XLA Modules:
  0.0 164.7 jit_solution(10670216536370425309)
XLA Ops:
  0.6 1.7 %collective-permute-start.2 = (bf16[256,512]{1,0:T(8,128)(2,1)}, bf16[256,512]{1,0:T(8,128)(2,1)}, u32[]{:S(2)}, u32[]{:S(2)}) collective-permute-start(bf16[256,512]{1,0:T(8,128)(2,1)} %refs_4_.1), channel_id=1, source_target_pairs={{0,4},{8,12},{16,20},{24,28},{32,36},{40,44},{48,52},{56,60},{64,6... | collective-permute-start | bytes 786440 | tf_op jit(solution)/shard_map/ppermute | solution.py:66
  2.4 5.3 %collective-permute-start = (bf16[256,512]{1,0:T(8,128)(2,1)}, bf16[256,512]{1,0:T(8,128)(2,1)}, u32[]{:S(2)}, u32[]{:S(2)}) collective-permute-start(bf16[256,512]{1,0:T(8,128)(2,1)} %refs_4_.1), channel_id=1, source_target_pairs={{4,8},{12,16},{20,24},{28,32},{36,40},{44,48},{52,56},{60,64},{68,... | collective-permute-start | bytes 786440 | tf_op jit(solution)/shard_map/ppermute | solution.py:66
  7.7 3.1 %collective-permute-start.1 = (bf16[256,512]{1,0:T(8,128)(2,1)}, bf16[256,512]{1,0:T(8,128)(2,1)}, u32[]{:S(2)}, u32[]{:S(2)}) collective-permute-start(bf16[256,512]{1,0:T(8,128)(2,1)} %refs_5_.1), channel_id=1, source_target_pairs={{4,8},{12,16},{20,24},{28,32},{36,40},{44,48},{52,56},{60,64},{68,... | collective-permute-start | bytes 786440 | tf_op jit(solution)/shard_map/ppermute | solution.py:66
  11.6 1.0 constant_dynamic-slice_fusion
  13.2 5.5 %collective-permute-start.4 = (bf16[256,512]{1,0:T(8,128)(2,1)}, bf16[256,512]{1,0:T(8,128)(2,1)S(1)}, u32[]{:S(2)}, u32[]{:S(2)}) collective-permute-start(bf16[256,512]{1,0:T(8,128)(2,1)} %collective-permute-done.2.refs_4_), channel_id=1, source_target_pairs={{4,8},{12,16},{20,24},{28,32},{36,40},{44,48},{52,56},{60,64},{68,... | collective-permute-start | bytes 786440 | tf_op jit(solution)/shard_map/ppermute | solution.py:66
  18.8 3.1 %collective-permute-start.5 = (bf16[256,512]{1,0:T(8,128)(2,1)}, bf16[256,512]{1,0:T(8,128)(2,1)S(1)}, u32[]{:S(2)}, u32[]{:S(2)}) collective-permute-start(bf16[256,512]{1,0:T(8,128)(2,1)} %collective-permute-done.3.refs_5_), channel_id=1, source_target_pairs={{4,8},{12,16},{20,24},{28,32},{36,40},{44,48},{52,56},{60,64},{68,... | collective-permute-start | bytes 786440 | tf_op jit(solution)/shard_map/ppermute | solution.py:66
  23.1 2.0 %collective-permute-done.4.refs_6_ = bf16[256,512]{1,0:T(8,128)(2,1)S(1)} collective-permute-done((bf16[256,512]{1,0:T(8,128)(2,1)}, bf16[256,512]{1,0:T(8,128)(2,1)S(1)}, u32[]{:S(2)}, u32[]{:S(2)}) %collective-permute-start.4) | collective-permute-done | bytes 262176 | tf_op jit(solution)/shard_map/ppermute | solution.py:66
  25.1 5.6 %collective-permute-done.5.refs_7_ = bf16[256,512]{1,0:T(8,128)(2,1)S(1)} collective-permute-done((bf16[256,512]{1,0:T(8,128)(2,1)}, bf16[256,512]{1,0:T(8,128)(2,1)S(1)}, u32[]{:S(2)}, u32[]{:S(2)}) %collective-permute-start.5) | collective-permute-done | bytes 262176 | tf_op jit(solution)/shard_map/ppermute | solution.py:66
  30.8 4.0 %shard_map.146 = (bf16[256,512]{1,0:T(8,128)(2,1)S(1)}, bf16[272,512]{1,0:T(8,128)(2,1)S(1)}, f32[256,128]{1,0:T(8,128)S(1)}) custom-call(s32[3]{0:T(128)S(1)} %pad_add_fusion.place, bf16[256,512]{1,0:T(8,128)(2,1)S(1)} %copy-done.35, bf16[256,512]{1,0:T(8,128)(2,1)S(1)} %copy-done.9, bf16[256,512]{1,0:T(8,128)(2,1)S(1)} %copy-done.10, ...), custom_call_target="tpu_custom_call" | custom-call | flops 1024 | bytes 1024 | tf_op jit(solution)/shard_map/pallas_call | solution.py:343
  34.8 2.3 %shard_map.147 = (bf16[128,4096]{1,0:T(8,128)(2,1)S(1)}, bf16[128,4096]{1,0:T(8,128)(2,1)}) custom-call(bf16[256,512]{1,0:T(8,128)(2,1)S(1)} %get-tuple-element.51.att_ref, bf16[512,4096]{1,0:T(8,128)(2,1)S(1)} %copy-done.2), custom_call_target="tpu_custom_call" | custom-call | flops 1024 | bytes 1024 | tf_op jit(solution)/shard_map/pallas_call | solution.py:354
  37.1 1.0 copy-done.15
  38.1 2.5 %collective-permute-start.8 = (bf16[128,4096]{1,0:T(8,128)(2,1)}, bf16[128,4096]{1,0:T(8,128)(2,1)}, u32[]{:S(2)}, u32[]{:S(2)}) collective-permute-start(bf16[128,4096]{1,0:T(8,128)(2,1)} %get-tuple-element.53), channel_id=1, source_target_pairs={{0,1},{1,0},{2,3},{3,2},{4,5},{5,4},{6,7},{7,6},{8,9},{9,8},{10,11... | collective-permute-start | bytes 3145736 | tf_op jit(solution)/shard_map/ppermute | solution.py:52
  40.6 1.7 %constant_dynamic-slice_fusion.2 = (bf16[2,1,64,4096]{3,2,1,0:T(8,128)(2,1)S(1)}, bf16[2,1,64,4096]{3,2,1,0:T(8,128)(2,1)S(1)}) fusion(bf16[2,2,64,4096]{3,2,1,0:T(8,128)(2,1)} %bitcast.37, s32[]{:T(128)S(6)} %select_n.49, s32[]{:T(128)S(6)} %select_n.50), kind=kLoop, calls=%fused_computation.28 | loop fusion | bytes 4194312 | tf_op jit(solution)/shard_map/dynamic_slice | solution.py:364
  43.5 1.5 add_convert_fusion.1.near_ref
  45.0 2.8 %collective-permute-start.9 = (bf16[128,4096]{1,0:T(8,128)(2,1)S(1)}, bf16[128,4096]{1,0:T(8,128)(2,1)S(1)}, u32[]{:S(2)}, u32[]{:S(2)}) collective-permute-start(bf16[128,4096]{1,0:T(8,128)(2,1)S(1)} %add_convert_fusion.1.near_ref), channel_id=1, source_target_pairs={{0,2},{2,0},{1,3},{3,1},{4,6},{6,4},{5,7},{7,5},{8,10},{10,8},{9,1... | collective-permute-start | bytes 3145736 | tf_op jit(solution)/shard_map/ppermute | solution.py:56
  47.8 5.9 %convolution_multiply_fusion.grad_ref = f32[256,1024]{1,0:T(8,128)S(1)} fusion(bf16[256,4096]{1,0:T(8,128)(2,1)S(1)} %pad_maximum_fusion, bf16[1024,4096]{1,0:T(8,128)(2,1)} %weight_ref.5, f32[1024]{0:T(1024)S(1)} %add_divide_fusion), kind=kOutput, calls=%fused_computation.14 | convolution fusion | flops 2147745792 | bytes 11538432 | tf_op jit(solution)/shard_map/dot_general | solution.py:48
  53.7 1.1 fusion
  54.9 1.8 %fusion.6.grad_copy_ref = f32[256,1024]{1,0:T(8,128)S(1)} fusion(f32[256,1024]{1,0:T(8,128)S(1)} %fusion, s32[1024]{0:T(1024)} %copy-done.46, f32[1024]{0:T(1024)S(1)} %copy-done.43, f32[256,1024]{1,0:T(8,128)S(1)} %convolution_multiply_fusion.grad_ref), kind=kOutput, calls=%fused_computation.13 | convolution fusion | flops 538705920 | bytes 3153920 | tf_op jit(solution)/shard_map/dot_general | solution.py:44
  56.7 14.6 %collective-permute-done.9.far_ref = bf16[128,4096]{1,0:T(8,128)(2,1)S(1)} collective-permute-done((bf16[128,4096]{1,0:T(8,128)(2,1)S(1)}, bf16[128,4096]{1,0:T(8,128)(2,1)S(1)}, u32[]{:S(2)}, u32[]{:S(2)}) %collective-permute-start.9) | collective-permute-done | bytes 1048608 | tf_op jit(solution)/shard_map/ppermute | solution.py:56
  71.4 1.2 shard_map.148
  74.0 5.3 %collective-permute-start.12 = (bf16[272,512]{1,0:T(8,128)(2,1)S(1)}, bf16[272,512]{1,0:T(8,128)(2,1)S(1)}, u32[]{:S(2)}, u32[]{:S(2)}) collective-permute-start(bf16[272,512]{1,0:T(8,128)(2,1)S(1)} %copy-done.13), channel_id=1, source_target_pairs={{4,8},{12,16},{20,24},{28,32},{36,40},{44,48},{52,56},{60,64},{68,... | collective-permute-start | bytes 835592 | tf_op jit(solution)/shard_map/ppermute | solution.py:66
  79.4 4.7 %shard_map.149 = (bf16[256,1024]{1,0:T(8,128)(2,1)S(1)}, bf16[256,1024]{1,0:T(8,128)(2,1)S(1)}) custom-call(bf16[128,4096]{1,0:T(8,128)(2,1)S(1)} %get-tuple-element.60.own_ref, bf16[128,4096]{1,0:T(8,128)(2,1)S(1)} %collective-permute-done.11.near_ref, bf16[4096,1024]{1,0:T(8,128)(2,1)S(1)} %bitcast.23, bf16[1024,1024]{1,0:T(8,128)(2,1)S(1)} %fusion.2.pick_ref, ...), custom_call_target="tpu_custom_call" | custom-call | flops 1024 | bytes 1024 | tf_op jit(solution)/shard_map/pallas_call | solution.py:398
  84.2 3.3 %shard_map.150 = (bf16[128,4096]{1,0:T(8,128)(2,1)S(1)}, bf16[128,4096]{1,0:T(8,128)(2,1)}) custom-call(bf16[256,1024]{1,0:T(8,128)(2,1)S(1)} %get-tuple-element.65.att_ref, bf16[1024,4096]{1,0:T(8,128)(2,1)S(1)} %bitcast.27), custom_call_target="tpu_custom_call" | custom-call | flops 1024 | bytes 1024 | tf_op jit(solution)/shard_map/pallas_call | solution.py:354
  87.5 1.0 copy-done.27
  88.4 2.4 %shard_map.151 = (bf16[128,4096]{1,0:T(8,128)(2,1)S(1)}, bf16[128,4096]{1,0:T(8,128)(2,1)S(1)}) custom-call(bf16[256,1024]{1,0:T(8,128)(2,1)S(1)} %get-tuple-element.69.hidden_grad_ref, bf16[4096,1024]{1,0:T(8,128)(2,1)S(1)} %bitcast.23), custom_call_target="tpu_custom_call" | custom-call | flops 1024 | bytes 1024 | tf_op jit(solution)/shard_map/pallas_call | solution.py:354
  91.4 2.3 %collective-permute-done.13 = bf16[128,4096]{1,0:T(8,128)(2,1)} collective-permute-done((bf16[128,4096]{1,0:T(8,128)(2,1)S(1)}, bf16[128,4096]{1,0:T(8,128)(2,1)}, u32[]{:S(2)}, u32[]{:S(2)}) %collective-permute-start.13) | collective-permute-done | bytes 1048608 | tf_op jit(solution)/shard_map/ppermute | solution.py:52
  93.7 1.5 add_convert_fusion.near_ref
  95.2 2.7 %collective-permute-start.14 = (bf16[128,4096]{1,0:T(8,128)(2,1)S(1)}, bf16[128,4096]{1,0:T(8,128)(2,1)S(1)}, u32[]{:S(2)}, u32[]{:S(2)}) collective-permute-start(bf16[128,4096]{1,0:T(8,128)(2,1)S(1)} %add_convert_fusion.near_ref), channel_id=1, source_target_pairs={{0,2},{2,0},{1,3},{3,1},{4,6},{6,4},{5,7},{7,5},{8,10},{10,8},{9,1... | collective-permute-start | bytes 3145736 | tf_op jit(solution)/shard_map/ppermute | solution.py:56
  97.9 1.8 %convert_add_fusion = f32[128,4096]{1,0:T(8,128)S(1)} fusion(bf16[128,4096]{1,0:T(8,128)(2,1)} %collective-permute-done.15, bf16[128,4096]{1,0:T(8,128)(2,1)} %copy-done.27), kind=kLoop, calls=%fused_computation.7 | loop fusion | flops 1572864 | bytes 4194304 | tf_op jit(solution)/shard_map/add | solution.py:357
  99.7 1.1 slice_select_fusion
  101.7 3.9 %collective-permute-done.16.refs_0_ = bf16[272,512]{1,0:T(8,128)(2,1)S(1)} collective-permute-done((bf16[272,512]{1,0:T(8,128)(2,1)S(1)}, bf16[272,512]{1,0:T(8,128)(2,1)S(1)}, u32[]{:S(2)}, u32[]{:S(2)}) %collective-permute-start.16) | collective-permute-done | bytes 278560 | tf_op jit(solution)/shard_map/ppermute | solution.py:66
  106.3 15.0 %collective-permute-done.14.far_ref = bf16[128,4096]{1,0:T(8,128)(2,1)S(1)} collective-permute-done((bf16[128,4096]{1,0:T(8,128)(2,1)S(1)}, bf16[128,4096]{1,0:T(8,128)(2,1)S(1)}, u32[]{:S(2)}, u32[]{:S(2)}) %collective-permute-start.14) | collective-permute-done | bytes 1048608 | tf_op jit(solution)/shard_map/ppermute | solution.py:56
  121.3 1.3 shard_map.152.low_ref
  122.6 1.1 collective-permute-start.18
  123.7 2.2 %copy-done.3 = bf16[512,4096]{1,0:T(8,128)(2,1)S(1)} copy-done((bf16[512,4096]{1,0:T(8,128)(2,1)S(1)}, bf16[512,4096]{1,0:T(8,128)(2,1)}, u32[]{:S(2)}) %copy-start.3) | copy-done | bytes 4194328
  125.9 1.5 shard_map.153.own_ref
  127.5 3.0 %collective-permute-start.17 = (bf16[64,4096]{1,0:T(8,128)(2,1)S(1)}, bf16[64,4096]{1,0:T(8,128)(2,1)S(1)}, u32[]{:S(2)}, u32[]{:S(2)}) collective-permute-start(bf16[64,4096]{1,0:T(8,128)(2,1)S(1)} %copy-done.45), channel_id=1, source_target_pairs={{0,2},{2,0},{1,3},{3,1},{4,6},{6,4},{5,7},{7,5},{8,10},{10,8},{9,1... | collective-permute-start | bytes 1572872 | tf_op jit(solution)/shard_map/ppermute | solution.py:56
  130.4 1.7 %shard_map.154 = (bf16[272,512]{1,0:T(8,128)(2,1)S(1)}, f32[256,128]{1,0:T(8,128)S(1)}) custom-call(bf16[128,512]{1,0:T(8,128)(2,1)S(1)} %shard_map.153.own_ref, bf16[128,4096]{1,0:T(8,128)(2,1)S(1)} %collective-permute-done.18.near_ref, bf16[512,4096]{1,0:T(8,128)(2,1)S(1)} %copy-done.4, bf16[256,512]{1,0:T(8,128)(2,1)S(1)} %copy-done.26), custom_call_target="tpu_custom_call" | custom-call | flops 1024 | bytes 1024 | tf_op jit(solution)/shard_map/pallas_call | solution.py:423
  132.1 4.2 %collective-permute-start.20 = (bf16[272,512]{1,0:T(8,128)(2,1)S(1)}, bf16[272,512]{1,0:T(8,128)(2,1)S(1)}, u32[]{:S(2)}, u32[]{:S(2)}) collective-permute-start(bf16[272,512]{1,0:T(8,128)(2,1)S(1)} %get-tuple-element.84.do_pack.refs_1_), channel_id=1, source_target_pairs={{4,8},{12,16},{20,24},{28,32},{36,40},{44,48},{52,56},{60,64},{68,... | collective-permute-start | bytes 835592 | tf_op jit(solution)/shard_map/ppermute | solution.py:66
  137.7 4.2 %collective-permute-start.22 = (bf16[272,512]{1,0:T(8,128)(2,1)S(1)}, bf16[272,512]{1,0:T(8,128)(2,1)S(1)}, u32[]{:S(2)}, u32[]{:S(2)}) collective-permute-start(bf16[272,512]{1,0:T(8,128)(2,1)S(1)} %copy-done.29), channel_id=1, source_target_pairs={{4,8},{12,16},{20,24},{28,32},{36,40},{44,48},{52,56},{60,64},{68,... | collective-permute-start | bytes 835592 | tf_op jit(solution)/shard_map/ppermute | solution.py:66
  142.0 1.1 dynamic-slice_convert_fusion
  143.1 1.9 %collective-permute-done.20.refs_5_ = bf16[272,512]{1,0:T(8,128)(2,1)S(1)} collective-permute-done((bf16[272,512]{1,0:T(8,128)(2,1)S(1)}, bf16[272,512]{1,0:T(8,128)(2,1)S(1)}, u32[]{:S(2)}, u32[]{:S(2)}) %collective-permute-start.20) | collective-permute-done | bytes 278560 | tf_op jit(solution)/shard_map/ppermute | solution.py:66
  145.0 4.2 %collective-permute-start.23 = (bf16[272,512]{1,0:T(8,128)(2,1)S(1)}, bf16[272,512]{1,0:T(8,128)(2,1)S(1)}, u32[]{:S(2)}, u32[]{:S(2)}) collective-permute-start(bf16[272,512]{1,0:T(8,128)(2,1)S(1)} %collective-permute-done.19.refs_3_), channel_id=1, source_target_pairs={{4,8},{12,16},{20,24},{28,32},{36,40},{44,48},{52,56},{60,64},{68,... | collective-permute-start | bytes 835592 | tf_op jit(solution)/shard_map/ppermute | solution.py:66
  149.3 2.7 %shard_map.156 = (f32[256,512]{1,0:T(8,128)S(1)}, f32[256,512]{1,0:T(8,128)S(1)}) custom-call(bf16[272,512]{1,0:T(8,128)(2,1)S(1)} %copy-done.14, bf16[272,512]{1,0:T(8,128)(2,1)S(1)} %get-tuple-element.84.do_pack.refs_1_, bf16[272,512]{1,0:T(8,128)(2,1)S(1)} %copy-done.29, bf16[272,512]{1,0:T(8,128)(2,1)S(1)} %collective-permute-done.19.refs_3_, ...), custom_call_target="tpu_custom_call" | custom-call | flops 1024 | bytes 1024 | tf_op jit(solution)/shard_map/pallas_call | solution.py:441
  152.1 5.9 %shard_map.155 = f32[256,512]{1,0:T(8,128)} custom-call(s32[3]{0:T(128)S(1)} %copy-done.42, bf16[272,512]{1,0:T(8,128)(2,1)S(1)} %copy-done.14, bf16[272,512]{1,0:T(8,128)(2,1)S(1)} %get-tuple-element.84.do_pack.refs_1_, f32[256,128]{1,0:T(8,128)S(1)} %get-tuple-element.85.lse_ref, f32[256,128]{1,0:T(8,128)S(1)} %get-tuple-element.86.delta_ref, ...), custom_call_target="tpu_custom_call" | custom-call | flops 1024 | bytes 1024 | tf_op jit(solution)/shard_map/pallas_call | solution.py:434
  158.0 2.7 %collective-permute-done.17 = bf16[64,4096]{1,0:T(8,128)(2,1)S(1)} collective-permute-done((bf16[64,4096]{1,0:T(8,128)(2,1)S(1)}, bf16[64,4096]{1,0:T(8,128)(2,1)S(1)}, u32[]{:S(2)}, u32[]{:S(2)}) %collective-permute-start.17) | collective-permute-done | bytes 524320 | tf_op jit(solution)/shard_map/ppermute | solution.py:56
  160.8 1.1 add_add_fusion
  161.9 2.8 %shard_map.157 = (f32[256,512]{1,0:T(8,128)}, f32[256,512]{1,0:T(8,128)}) custom-call(bf16[272,512]{1,0:T(8,128)(2,1)S(1)} %copy-done.34, bf16[272,512]{1,0:T(8,128)(2,1)S(1)} %collective-permute-done.21.refs_1_, bf16[272,512]{1,0:T(8,128)(2,1)S(1)} %collective-permute-done.22.refs_2_, bf16[272,512]{1,0:T(8,128)(2,1)S(1)} %collective-permute-done.23.refs_3_, ...), custom_call_target="tpu_custom_call" | custom-call | flops 1024 | bytes 1024 | tf_op jit(solution)/shard_map/pallas_call | solution.py:441
  (137 shorter events, 9.2 us)
Async XLA Ops:
  0.6 10.9 %copy-start = (bf16[256,4096]{1,0:T(8,128)(2,1)S(1)}, bf16[256,4096]{1,0:T(8,128)(2,1)}, u32[]{:S(2)}) copy-start(bf16[256,4096]{1,0:T(8,128)(2,1)} %param.14) | copy-start | bytes 6291460
  0.6 12.6 %collective-permute-start.2 = (bf16[256,512]{1,0:T(8,128)(2,1)}, bf16[256,512]{1,0:T(8,128)(2,1)}, u32[]{:S(2)}, u32[]{:S(2)}) collective-permute-start(bf16[256,512]{1,0:T(8,128)(2,1)} %refs_4_.1), channel_id=1, source_target_pairs={{0,4},{8,12},{16,20},{24,28},{32,36},{40,44},{48,52},{56,60},{64,6... | collective-permute-start | bytes 786440 | tf_op jit(solution)/shard_map/ppermute | solution.py:66
  2.4 16.3 %collective-permute-start = (bf16[256,512]{1,0:T(8,128)(2,1)}, bf16[256,512]{1,0:T(8,128)(2,1)}, u32[]{:S(2)}, u32[]{:S(2)}) collective-permute-start(bf16[256,512]{1,0:T(8,128)(2,1)} %refs_4_.1), channel_id=1, source_target_pairs={{4,8},{12,16},{20,24},{28,32},{36,40},{44,48},{52,56},{60,64},{68,... | collective-permute-start | bytes 786440 | tf_op jit(solution)/shard_map/ppermute | solution.py:66
  7.6 11.2 %collective-permute-start.3 = (bf16[256,512]{1,0:T(8,128)(2,1)}, bf16[256,512]{1,0:T(8,128)(2,1)}, u32[]{:S(2)}, u32[]{:S(2)}) collective-permute-start(bf16[256,512]{1,0:T(8,128)(2,1)} %refs_5_.1), channel_id=1, source_target_pairs={{0,4},{8,12},{16,20},{24,28},{32,36},{40,44},{48,52},{56,60},{64,6... | collective-permute-start | bytes 786440 | tf_op jit(solution)/shard_map/ppermute | solution.py:66
  7.7 14.2 %collective-permute-start.1 = (bf16[256,512]{1,0:T(8,128)(2,1)}, bf16[256,512]{1,0:T(8,128)(2,1)}, u32[]{:S(2)}, u32[]{:S(2)}) collective-permute-start(bf16[256,512]{1,0:T(8,128)(2,1)} %refs_5_.1), channel_id=1, source_target_pairs={{4,8},{12,16},{20,24},{28,32},{36,40},{44,48},{52,56},{60,64},{68,... | collective-permute-start | bytes 786440 | tf_op jit(solution)/shard_map/ppermute | solution.py:66
  11.6 42.2 %copy-start.46 = (s32[1024]{0:T(1024)}, s32[1024]{0:T(1024)S(1)}, u32[]{:S(2)}) copy-start(s32[1024]{0:T(1024)S(1)} %broadcast_subtract_fusion) | copy-start | bytes 12292
  11.6 19.2 %copy-start.9 = (bf16[256,512]{1,0:T(8,128)(2,1)S(1)}, bf16[256,512]{1,0:T(8,128)(2,1)}, u32[]{:S(2)}) copy-start(bf16[256,512]{1,0:T(8,128)(2,1)} %refs_4_.1) | copy-start | bytes 786436
  11.6 19.2 %copy-start.10 = (bf16[256,512]{1,0:T(8,128)(2,1)S(1)}, bf16[256,512]{1,0:T(8,128)(2,1)}, u32[]{:S(2)}) copy-start(bf16[256,512]{1,0:T(8,128)(2,1)} %refs_5_.1) | copy-start | bytes 786436
  11.6 19.2 %copy-start.35 = (bf16[256,512]{1,0:T(8,128)(2,1)S(1)}, bf16[256,512]{1,0:T(8,128)(2,1)}, u32[]{:S(2)}) copy-start(bf16[256,512]{1,0:T(8,128)(2,1)} %q_ref.1) | copy-start | bytes 786436
  12.7 22.0 %copy-start.41 = (s32[3]{0:T(128)}, s32[3]{0:T(128)S(1)}, u32[]{:S(2)}) copy-start(s32[3]{0:T(128)S(1)} %pad_add_fusion.place) | copy-start | bytes 40
  13.2 21.6 %copy-start.2 = (bf16[512,4096]{1,0:T(8,128)(2,1)S(1)}, bf16[512,4096]{1,0:T(8,128)(2,1)}, u32[]{:S(2)}) copy-start(bf16[512,4096]{1,0:T(8,128)(2,1)} %weight_ref.7) | copy-start | bytes 12582916
  13.2 11.9 %collective-permute-start.4 = (bf16[256,512]{1,0:T(8,128)(2,1)}, bf16[256,512]{1,0:T(8,128)(2,1)S(1)}, u32[]{:S(2)}, u32[]{:S(2)}) collective-permute-start(bf16[256,512]{1,0:T(8,128)(2,1)} %collective-permute-done.2.refs_4_), channel_id=1, source_target_pairs={{4,8},{12,16},{20,24},{28,32},{36,40},{44,48},{52,56},{60,64},{68,... | collective-permute-start | bytes 786440 | tf_op jit(solution)/shard_map/ppermute | solution.py:66
  18.7 6.4 %collective-permute-start.6 = (bf16[256,512]{1,0:T(8,128)(2,1)}, bf16[256,512]{1,0:T(8,128)(2,1)S(1)}, u32[]{:S(2)}, u32[]{:S(2)}) collective-permute-start(bf16[256,512]{1,0:T(8,128)(2,1)} %collective-permute-done.refs_2_), channel_id=1, source_target_pairs={{0,4},{8,12},{16,20},{24,28},{32,36},{40,44},{48,52},{56,60},{64,6... | collective-permute-start | bytes 786440 | tf_op jit(solution)/shard_map/ppermute | solution.py:66
  18.8 11.9 %collective-permute-start.5 = (bf16[256,512]{1,0:T(8,128)(2,1)}, bf16[256,512]{1,0:T(8,128)(2,1)S(1)}, u32[]{:S(2)}, u32[]{:S(2)}) collective-permute-start(bf16[256,512]{1,0:T(8,128)(2,1)} %collective-permute-done.3.refs_5_), channel_id=1, source_target_pairs={{4,8},{12,16},{20,24},{28,32},{36,40},{44,48},{52,56},{60,64},{68,... | collective-permute-start | bytes 786440 | tf_op jit(solution)/shard_map/ppermute | solution.py:66
  21.9 8.8 %collective-permute-start.7 = (bf16[256,512]{1,0:T(8,128)(2,1)}, bf16[256,512]{1,0:T(8,128)(2,1)S(1)}, u32[]{:S(2)}, u32[]{:S(2)}) collective-permute-start(bf16[256,512]{1,0:T(8,128)(2,1)} %collective-permute-done.1.refs_3_), channel_id=1, source_target_pairs={{0,4},{8,12},{16,20},{24,28},{32,36},{40,44},{48,52},{56,60},{64,6... | collective-permute-start | bytes 786440 | tf_op jit(solution)/shard_map/ppermute | solution.py:66
  38.1 5.1 %collective-permute-start.8 = (bf16[128,4096]{1,0:T(8,128)(2,1)}, bf16[128,4096]{1,0:T(8,128)(2,1)}, u32[]{:S(2)}, u32[]{:S(2)}) collective-permute-start(bf16[128,4096]{1,0:T(8,128)(2,1)} %get-tuple-element.53), channel_id=1, source_target_pairs={{0,1},{1,0},{2,3},{3,2},{4,5},{5,4},{6,7},{7,6},{8,9},{9,8},{10,11... | collective-permute-start | bytes 3145736 | tf_op jit(solution)/shard_map/ppermute | solution.py:52
  45.0 26.3 %collective-permute-start.9 = (bf16[128,4096]{1,0:T(8,128)(2,1)S(1)}, bf16[128,4096]{1,0:T(8,128)(2,1)S(1)}, u32[]{:S(2)}, u32[]{:S(2)}) collective-permute-start(bf16[128,4096]{1,0:T(8,128)(2,1)S(1)} %add_convert_fusion.1.near_ref), channel_id=1, source_target_pairs={{0,2},{2,0},{1,3},{3,1},{4,6},{6,4},{5,7},{7,5},{8,10},{10,8},{9,1... | collective-permute-start | bytes 3145736 | tf_op jit(solution)/shard_map/ppermute | solution.py:56
  47.8 31.5 %slice-start = ((s8[8388608]{0:T(1024)(128)(4,1)}), s8[4194304]{0:T(1024)(128)(4,1)S(1)}, s32[]{:S(2)}) async-start(s8[8388608]{0:T(1024)(128)(4,1)} %bitcast.22), calls=%async_computation | async-start | bytes 8388608
  47.8 31.5 %slice-start.1 = ((s8[8388608]{0:T(1024)(128)(4,1)}), s8[4194304]{0:T(1024)(128)(4,1)S(1)}, s32[]{:S(2)}) async-start(s8[8388608]{0:T(1024)(128)(4,1)} %bitcast.22), calls=%async_computation.1 | async-start | bytes 8388608
  47.8 23.5 %collective-permute-start.10 = (bf16[272,512]{1,0:T(8,128)(2,1)S(1)}, bf16[272,512]{1,0:T(8,128)(2,1)S(1)}, u32[]{:S(2)}, u32[]{:S(2)}) collective-permute-start(bf16[272,512]{1,0:T(8,128)(2,1)S(1)} %copy-done.13), channel_id=1, source_target_pairs={{0,4},{8,12},{16,20},{24,28},{32,36},{40,44},{48,52},{56,60},{64,6... | collective-permute-start | bytes 835592 | tf_op jit(solution)/shard_map/ppermute | solution.py:66
  54.9 16.5 %copy-start.8 = (bf16[2,1,64,4096]{3,2,1,0:T(8,128)(2,1)S(1)}, bf16[2,1,64,4096]{3,2,1,0:T(8,128)(2,1)}, u32[]{:S(2)}) copy-start(bf16[2,1,64,4096]{3,2,1,0:T(8,128)(2,1)} %constant_dynamic-slice_fusion) | copy-start | bytes 3145732
  54.9 16.5 %copy-start.36 = (f32[4096]{0:T(1024)S(1)}, f32[4096]{0:T(1024)}, u32[]{:S(2)}) copy-start(f32[4096]{0:T(1024)} %param.16) | copy-start | bytes 49156
  56.7 22.7 %copy-start.40 = (f32[1024]{0:T(1024)S(1)}, f32[1024]{0:T(1024)}, u32[]{:S(2)}) copy-start(f32[1024]{0:T(1024)} %copy-done.39) | copy-start | bytes 12292
  71.3 12.8 %slice-start.2 = ((s8[8388608]{0:T(1024)(128)(4,1)}), s8[4194304]{0:T(1024)(128)(4,1)S(1)}, s32[]{:S(2)}) async-start(s8[8388608]{0:T(1024)(128)(4,1)} %bitcast.26), calls=%async_computation.2 | async-start | bytes 8388608
  73.2 10.9 %copy-start.5 = (f32[128,4096]{1,0:T(8,128)}, f32[128,4096]{1,0:T(8,128)S(1)}, u32[]{:S(2)}) copy-start(f32[128,4096]{1,0:T(8,128)S(1)} %get-tuple-element.59.unit_ref) | copy-start | bytes 6291460
  73.2 6.1 %collective-permute-start.11 = (bf16[128,4096]{1,0:T(8,128)(2,1)S(1)}, bf16[128,4096]{1,0:T(8,128)(2,1)S(1)}, u32[]{:S(2)}, u32[]{:S(2)}) collective-permute-start(bf16[128,4096]{1,0:T(8,128)(2,1)S(1)} %get-tuple-element.60.own_ref), channel_id=1, source_target_pairs={{0,1},{1,0},{2,3},{3,2},{4,5},{5,4},{6,7},{7,6},{8,9},{9,8},{10,11... | collective-permute-start | bytes 3145736 | tf_op jit(solution)/shard_map/ppermute | solution.py:52
  74.0 13.5 %collective-permute-start.12 = (bf16[272,512]{1,0:T(8,128)(2,1)S(1)}, bf16[272,512]{1,0:T(8,128)(2,1)S(1)}, u32[]{:S(2)}, u32[]{:S(2)}) collective-permute-start(bf16[272,512]{1,0:T(8,128)(2,1)S(1)} %copy-done.13), channel_id=1, source_target_pairs={{4,8},{12,16},{20,24},{28,32},{36,40},{44,48},{52,56},{60,64},{68,... | collective-permute-start | bytes 835592 | tf_op jit(solution)/shard_map/ppermute | solution.py:66
  90.8 2.9 %collective-permute-start.13 = (bf16[128,4096]{1,0:T(8,128)(2,1)S(1)}, bf16[128,4096]{1,0:T(8,128)(2,1)}, u32[]{:S(2)}, u32[]{:S(2)}) collective-permute-start(bf16[128,4096]{1,0:T(8,128)(2,1)S(1)} %get-tuple-element.71), channel_id=1, source_target_pairs={{0,1},{1,0},{2,3},{3,2},{4,5},{5,4},{6,7},{7,6},{8,9},{9,8},{10,11... | collective-permute-start | bytes 3145736 | tf_op jit(solution)/shard_map/ppermute | solution.py:52
  91.2 6.7 %collective-permute-start.15 = (bf16[128,4096]{1,0:T(8,128)(2,1)}, bf16[128,4096]{1,0:T(8,128)(2,1)}, u32[]{:S(2)}, u32[]{:S(2)}) collective-permute-start(bf16[128,4096]{1,0:T(8,128)(2,1)} %get-tuple-element.73), channel_id=1, source_target_pairs={{0,1},{1,0},{2,3},{3,2},{4,5},{5,4},{6,7},{7,6},{8,9},{9,8},{10,11... | collective-permute-start | bytes 3145736 | tf_op jit(solution)/shard_map/ppermute | solution.py:52
  95.2 26.1 %collective-permute-start.14 = (bf16[128,4096]{1,0:T(8,128)(2,1)S(1)}, bf16[128,4096]{1,0:T(8,128)(2,1)S(1)}, u32[]{:S(2)}, u32[]{:S(2)}) collective-permute-start(bf16[128,4096]{1,0:T(8,128)(2,1)S(1)} %add_convert_fusion.near_ref), channel_id=1, source_target_pairs={{0,2},{2,0},{1,3},{3,1},{4,6},{6,4},{5,7},{7,5},{8,10},{10,8},{9,1... | collective-permute-start | bytes 3145736 | tf_op jit(solution)/shard_map/ppermute | solution.py:56
  97.9 7.7 %collective-permute-start.16 = (bf16[272,512]{1,0:T(8,128)(2,1)S(1)}, bf16[272,512]{1,0:T(8,128)(2,1)S(1)}, u32[]{:S(2)}, u32[]{:S(2)}) collective-permute-start(bf16[272,512]{1,0:T(8,128)(2,1)S(1)} %copy-done.31), channel_id=1, source_target_pairs={{0,4},{8,12},{16,20},{24,28},{32,36},{40,44},{48,52},{56,60},{64,6... | collective-permute-start | bytes 835592 | tf_op jit(solution)/shard_map/ppermute | solution.py:66
  99.7 21.6 %copy-start.6 = (f32[128,4096]{1,0:T(8,128)S(1)}, f32[128,4096]{1,0:T(8,128)}, u32[]{:S(2)}) copy-start(f32[128,4096]{1,0:T(8,128)} %copy-done.5) | copy-start | bytes 6291460
  99.7 21.6 %copy-start.38 = (f32[128,128]{1,0:T(8,128)S(1)}, f32[128,128]{1,0:T(8,128)}, u32[]{:S(2)}) copy-start(f32[128,128]{1,0:T(8,128)} %copy-done.37) | copy-start | bytes 196612
  122.6 7.8 %collective-permute-start.18 = (bf16[128,4096]{1,0:T(8,128)(2,1)S(1)}, bf16[128,4096]{1,0:T(8,128)(2,1)S(1)}, u32[]{:S(2)}, u32[]{:S(2)}) collective-permute-start(bf16[128,4096]{1,0:T(8,128)(2,1)S(1)} %shard_map.152.low_ref), channel_id=1, source_target_pairs={{0,1},{1,0},{2,3},{3,2},{4,5},{5,4},{6,7},{7,6},{8,9},{9,8},{10,11... | collective-permute-start | bytes 3145736 | tf_op jit(solution)/shard_map/ppermute | solution.py:52
  127.5 33.3 %collective-permute-start.17 = (bf16[64,4096]{1,0:T(8,128)(2,1)S(1)}, bf16[64,4096]{1,0:T(8,128)(2,1)S(1)}, u32[]{:S(2)}, u32[]{:S(2)}) collective-permute-start(bf16[64,4096]{1,0:T(8,128)(2,1)S(1)} %copy-done.45), channel_id=1, source_target_pairs={{0,2},{2,0},{1,3},{3,1},{4,6},{6,4},{5,7},{7,5},{8,10},{10,8},{9,1... | collective-permute-start | bytes 1572872 | tf_op jit(solution)/shard_map/ppermute | solution.py:56
  132.1 12.9 %collective-permute-start.20 = (bf16[272,512]{1,0:T(8,128)(2,1)S(1)}, bf16[272,512]{1,0:T(8,128)(2,1)S(1)}, u32[]{:S(2)}, u32[]{:S(2)}) collective-permute-start(bf16[272,512]{1,0:T(8,128)(2,1)S(1)} %get-tuple-element.84.do_pack.refs_1_), channel_id=1, source_target_pairs={{4,8},{12,16},{20,24},{28,32},{36,40},{44,48},{52,56},{60,64},{68,... | collective-permute-start | bytes 835592 | tf_op jit(solution)/shard_map/ppermute | solution.py:66
  136.3 8.7 %collective-permute-start.19 = (bf16[272,512]{1,0:T(8,128)(2,1)S(1)}, bf16[272,512]{1,0:T(8,128)(2,1)S(1)}, u32[]{:S(2)}, u32[]{:S(2)}) collective-permute-start(bf16[272,512]{1,0:T(8,128)(2,1)S(1)} %get-tuple-element.84.do_pack.refs_1_), channel_id=1, source_target_pairs={{0,4},{8,12},{16,20},{24,28},{32,36},{40,44},{48,52},{56,60},{64,6... | collective-permute-start | bytes 835592 | tf_op jit(solution)/shard_map/ppermute | solution.py:66
  136.8 12.5 %copy-start.11 = (bf16[256,512]{1,0:T(8,128)(2,1)S(1)}, bf16[256,512]{1,0:T(8,128)(2,1)}, u32[]{:S(2)}) copy-start(bf16[256,512]{1,0:T(8,128)(2,1)} %refs_5_.1) | copy-start | bytes 786436
  136.8 12.5 %copy-start.14 = (bf16[272,512]{1,0:T(8,128)(2,1)S(1)}, bf16[272,512]{1,0:T(8,128)(2,1)}, u32[]{:S(2)}) copy-start(bf16[272,512]{1,0:T(8,128)(2,1)} %copy-done.12) | copy-start | bytes 835588
  136.8 12.5 %copy-start.32 = (bf16[272,512]{1,0:T(8,128)(2,1)S(1)}, bf16[272,512]{1,0:T(8,128)(2,1)}, u32[]{:S(2)}) copy-start(bf16[272,512]{1,0:T(8,128)(2,1)} %copy-done.30) | copy-start | bytes 835588
  137.7 14.3 %copy-start.18 = (bf16[256,512]{1,0:T(8,128)(2,1)S(1)}, bf16[256,512]{1,0:T(8,128)(2,1)}, u32[]{:S(2)}) copy-start(bf16[256,512]{1,0:T(8,128)(2,1)} %copy-done.17) | copy-start | bytes 786436
  137.7 14.3 %copy-start.20 = (bf16[256,512]{1,0:T(8,128)(2,1)S(1)}, bf16[256,512]{1,0:T(8,128)(2,1)}, u32[]{:S(2)}) copy-start(bf16[256,512]{1,0:T(8,128)(2,1)} %copy-done.19) | copy-start | bytes 786436
  137.7 14.3 %copy-start.22 = (bf16[256,512]{1,0:T(8,128)(2,1)S(1)}, bf16[256,512]{1,0:T(8,128)(2,1)}, u32[]{:S(2)}) copy-start(bf16[256,512]{1,0:T(8,128)(2,1)} %copy-done.21) | copy-start | bytes 786436
  137.7 14.3 %copy-start.24 = (bf16[256,512]{1,0:T(8,128)(2,1)S(1)}, bf16[256,512]{1,0:T(8,128)(2,1)}, u32[]{:S(2)}) copy-start(bf16[256,512]{1,0:T(8,128)(2,1)} %copy-done.23) | copy-start | bytes 786436
  137.7 14.3 %copy-start.42 = (s32[3]{0:T(128)S(1)}, s32[3]{0:T(128)}, u32[]{:S(2)}) copy-start(s32[3]{0:T(128)} %copy-done.41) | copy-start | bytes 40
  137.7 24.1 %collective-permute-start.22 = (bf16[272,512]{1,0:T(8,128)(2,1)S(1)}, bf16[272,512]{1,0:T(8,128)(2,1)S(1)}, u32[]{:S(2)}, u32[]{:S(2)}) collective-permute-start(bf16[272,512]{1,0:T(8,128)(2,1)S(1)} %copy-done.29), channel_id=1, source_target_pairs={{4,8},{12,16},{20,24},{28,32},{36,40},{44,48},{52,56},{60,64},{68,... | collective-permute-start | bytes 835592 | tf_op jit(solution)/shard_map/ppermute | solution.py:66
  145.0 16.9 %collective-permute-start.23 = (bf16[272,512]{1,0:T(8,128)(2,1)S(1)}, bf16[272,512]{1,0:T(8,128)(2,1)S(1)}, u32[]{:S(2)}, u32[]{:S(2)}) collective-permute-start(bf16[272,512]{1,0:T(8,128)(2,1)S(1)} %collective-permute-done.19.refs_3_), channel_id=1, source_target_pairs={{4,8},{12,16},{20,24},{28,32},{36,40},{44,48},{52,56},{60,64},{68,... | collective-permute-start | bytes 835592 | tf_op jit(solution)/shard_map/ppermute | solution.py:66
  149.2 12.7 %collective-permute-start.21 = (bf16[272,512]{1,0:T(8,128)(2,1)S(1)}, bf16[272,512]{1,0:T(8,128)(2,1)S(1)}, u32[]{:S(2)}, u32[]{:S(2)}) collective-permute-start(bf16[272,512]{1,0:T(8,128)(2,1)S(1)} %collective-permute-done.20.refs_5_), channel_id=1, source_target_pairs={{0,4},{8,12},{16,20},{24,28},{32,36},{40,44},{48,52},{56,60},{64,6... | collective-permute-start | bytes 835592 | tf_op jit(solution)/shard_map/ppermute | solution.py:66
  (27 other events, 114.1 us)
